TPU v7x, 32 devices: a whole 2x2x4 slice. The times are simulated.
32 devices in a mesh: dp: 16 (over z, x, core), tensor: 2 (over y).
Axes of the slice: x: 2, y: 2, z: 4, core: 2. Of those that a mesh axis runs over, the one named last changes fastest.
Arguments:
- tokens: bfloat16 [32768, 1024], P(('dp', 'tensor')), may hold values from -6 to 6
- cotangent: bfloat16 [32768, 1024], P(('dp', 'tensor')), may hold values from -6 to 6
- w_qkv: bfloat16 [3, 1024, 1024], P(None, None, 'tensor'), may hold values from -0.1875 to 0.1875
- bias_q: float32 [1024], P('tensor'), may hold values from -2 to 2
- bias_v: float32 [1024], P('tensor'), may hold values from -2 to 2
- w_out: bfloat16 [1024, 1024], P('tensor'), may hold values from -3 to 3
- bias_o: float32 [1024], replicated, may hold values from -2 to 2
- gain_one: float32 [1024], replicated, may hold values from 0.25 to 1.75
- shift_one: float32 [1024], replicated, may hold values from -2 to 2
- w_up: bfloat16 [1024, 4096], P(None, 'tensor'), may hold values from -0.1875 to 0.1875
- bias_up: float32 [4096], P('tensor'), may hold values from -2 to 2
- w_down: bfloat16 [4096, 1024], P('tensor'), may hold values from -0.09375 to 0.09375
- bias_down: float32 [1024], replicated, may hold values from -2 to 2
- gain_two: float32 [1024], replicated, may hold values from 0.25 to 1.75
- shift_two: float32 [1024], replicated, may hold values from -2 to 2
Outputs:
- output: bfloat16 [32768, 1024], P(('dp', 'tensor'))
- grad_input: float32 [32768, 1024], P(('dp', 'tensor'))
- grad_qkv: float32 [3, 1024, 1024], P(None, 'dp', 'tensor')
- grad_bias_q: float32 [1024], replicated
- grad_bias_v: float32 [1024], replicated
- grad_out: float32 [1024, 1024], P('tensor', 'dp')
- grad_bias_o: float32 [1024], replicated
- grad_gain_one: float32 [1024], replicated
- grad_shift_one: float32 [1024], replicated
- grad_up: float32 [1024, 4096], P('dp', 'tensor')
- grad_bias_up: float32 [4096], replicated
- grad_down: float32 [4096, 1024], P('tensor', 'dp')
- grad_bias_down: float32 [1024], replicated
- grad_gain_two: float32 [1024], replicated
- grad_shift_two: float32 [1024], replicated
All inputs are finite; a program needn't handle non-finite values.
Results may differ from a plain program's by a relative error of at most 0.019.
Values may be sent and summed in bfloat16 or wider, within the bound.
A program may use at most 192 MiB of HBM per device.

v0:
```python
import jax
import jax.numpy as jnp
from jax import lax
from jax.sharding import PartitionSpec as P

D = 1024
FF = 4096
HEAD_DIM = 64
SEQ = 512


def gelu_pair(inner_pre):
    normal_cdf = 0.5 * (1.0 + jax.scipy.special.erf(inner_pre * 0.7071067811865476))
    density = jnp.exp(-0.5 * inner_pre * inner_pre) * 0.3989422804014327
    return (inner_pre * normal_cdf, normal_cdf + inner_pre * density)


def norm_forward(summed, gain, shift):
    centre = summed - jnp.mean(summed, axis=-1, keepdims=True)
    scaled = lax.rsqrt(jnp.mean(centre * centre, axis=-1, keepdims=True) + 1e-05)
    normed = centre * scaled
    return (normed * gain + shift, normed, scaled)


def norm_backward(upstream, gain, normed, scaled):
    grad_norm = upstream * gain
    return scaled * (
        grad_norm
        - jnp.mean(grad_norm, axis=-1, keepdims=True)
        - normed * jnp.mean(grad_norm * normed, axis=-1, keepdims=True)
    )


def attend_block(block):
    queries, key_rows, values = block
    scores = jnp.einsum(
        "qhd,khd->hqk", queries, key_rows, preferred_element_type=jnp.float32
    ) * HEAD_DIM ** (-0.5)
    peak_score = jnp.max(scores, axis=-1, keepdims=True)
    lifted = jnp.exp(scores - peak_score)
    totals = jnp.sum(lifted, axis=-1, keepdims=True)
    weights = (lifted / totals).astype(jnp.bfloat16)
    context = jnp.einsum("hqk,khd->qhd", weights, values, preferred_element_type=jnp.float32)
    return (context.astype(jnp.bfloat16), (peak_score + jnp.log(totals))[..., 0])


def attend_back(block):
    queries, key_rows, values, logsum, grad_ctx = block
    scale = HEAD_DIM ** (-0.5)
    scores = (
        jnp.einsum("qhd,khd->hqk", queries, key_rows, preferred_element_type=jnp.float32) * scale
    )
    weights = jnp.exp(scores - logsum[..., None])
    grad_weights = jnp.einsum("qhd,khd->hqk", grad_ctx, values, preferred_element_type=jnp.float32)
    grad_scores = weights * (grad_weights - jnp.sum(weights * grad_weights, axis=-1, keepdims=True))
    grad_low = grad_scores.astype(jnp.bfloat16)
    grad_v = jnp.einsum(
        "hqk,qhd->khd", weights.astype(jnp.bfloat16), grad_ctx, preferred_element_type=jnp.float32
    )
    grad_q = (
        jnp.einsum("hqk,khd->qhd", grad_low, key_rows, preferred_element_type=jnp.float32) * scale
    )
    grad_k = (
        jnp.einsum("hqk,qhd->khd", grad_low, queries, preferred_element_type=jnp.float32) * scale
    )
    return (grad_q.astype(jnp.bfloat16), grad_k.astype(jnp.bfloat16), grad_v.astype(jnp.bfloat16))


def body(
    tokens,
    cotangent,
    w_qkv,
    bias_q,
    bias_v,
    w_out,
    bias_o,
    gain_one,
    shift_one,
    w_up,
    bias_up,
    w_down,
    bias_down,
    gain_two,
    shift_two,
):
    rank = lax.axis_index("tensor")
    full_rows = lax.all_gather(tokens, "tensor", axis=0, tiled=True)
    group_rows = full_rows.shape[0]
    local_width = w_qkv.shape[2]
    head_shape = (group_rows // SEQ, SEQ, local_width // HEAD_DIM, HEAD_DIM)
    projected = jnp.einsum("td,kde->kte", full_rows, w_qkv, preferred_element_type=jnp.float32)
    queries = (projected[0] + bias_q).astype(jnp.bfloat16).reshape(head_shape)
    key_rows = projected[1].astype(jnp.bfloat16).reshape(head_shape)
    values = (projected[2] + bias_v).astype(jnp.bfloat16).reshape(head_shape)
    context, logsum = lax.map(attend_block, (queries, key_rows, values))
    context = context.reshape(group_rows, local_width)
    attended = (
        lax.psum_scatter(
            jnp.dot(context, w_out, preferred_element_type=jnp.float32),
            "tensor",
            scatter_dimension=0,
            tiled=True,
        )
        + bias_o
    )
    hidden_one, normed_one, scaled_one = norm_forward(
        tokens.astype(jnp.float32) + attended, gain_one, shift_one
    )
    hidden_rows = lax.all_gather(hidden_one.astype(jnp.bfloat16), "tensor", axis=0, tiled=True)
    inner_pre = jnp.dot(hidden_rows, w_up, preferred_element_type=jnp.float32) + bias_up
    activated, slope = gelu_pair(inner_pre)
    active_low = activated.astype(jnp.bfloat16)
    branch = (
        lax.psum_scatter(
            jnp.dot(active_low, w_down, preferred_element_type=jnp.float32),
            "tensor",
            scatter_dimension=0,
            tiled=True,
        )
        + bias_down
    )
    result, normed_two, scaled_two = norm_forward(hidden_one + branch, gain_two, shift_two)
    upstream = cotangent.astype(jnp.float32)
    grad_two = norm_backward(upstream, gain_two, normed_two, scaled_two)
    grad_branch = grad_two.astype(jnp.bfloat16)
    branch_rows = lax.all_gather(grad_branch, "tensor", axis=0, tiled=True)
    grad_down = jnp.einsum("tf,td->fd", active_low, branch_rows, preferred_element_type=jnp.float32)
    grad_inner = (
        jnp.einsum("td,fd->tf", branch_rows, w_down, preferred_element_type=jnp.float32) * slope
    ).astype(jnp.bfloat16)
    grad_up = jnp.einsum("td,tf->df", hidden_rows, grad_inner, preferred_element_type=jnp.float32)
    grad_hidden = grad_two + lax.psum_scatter(
        jnp.einsum("tf,df->td", grad_inner, w_up, preferred_element_type=jnp.float32),
        "tensor",
        scatter_dimension=0,
        tiled=True,
    )
    grad_one = norm_backward(grad_hidden, gain_one, normed_one, scaled_one)
    grad_attended = grad_one.astype(jnp.bfloat16)
    attended_rows = lax.all_gather(grad_attended, "tensor", axis=0, tiled=True)
    grad_out = jnp.einsum("te,td->ed", context, attended_rows, preferred_element_type=jnp.float32)
    grad_context = jnp.einsum(
        "td,ed->te", attended_rows, w_out, preferred_element_type=jnp.float32
    ).astype(jnp.bfloat16)
    grad_q, grad_k, grad_v = lax.map(
        attend_back, (queries, key_rows, values, logsum, grad_context.reshape(head_shape))
    )
    grad_stack = jnp.stack(
        [
            grad_q.reshape(group_rows, local_width),
            grad_k.reshape(group_rows, local_width),
            grad_v.reshape(group_rows, local_width),
        ]
    )
    weight_qkv = jnp.einsum(
        "td,kte->kde", full_rows, grad_stack, preferred_element_type=jnp.float32
    )
    grad_input = grad_one + lax.psum_scatter(
        jnp.einsum("kte,kde->td", grad_stack, w_qkv, preferred_element_type=jnp.float32).astype(
            jnp.bfloat16
        ),
        "tensor",
        scatter_dimension=0,
        tiled=True,
    ).astype(jnp.float32)

    def placed(piece, length):
        return lax.dynamic_update_slice_in_dim(
            jnp.zeros((length,), jnp.float32), piece, rank * piece.shape[0], 0
        )

    vectors = lax.psum(
        (
            placed(jnp.sum(grad_stack[0].astype(jnp.float32), axis=0), D),
            placed(jnp.sum(grad_stack[2].astype(jnp.float32), axis=0), D),
            jnp.sum(grad_attended.astype(jnp.float32), axis=0),
            jnp.sum(grad_hidden * normed_one, axis=0),
            jnp.sum(grad_hidden, axis=0),
            placed(jnp.sum(grad_inner.astype(jnp.float32), axis=0), FF),
            jnp.sum(grad_branch.astype(jnp.float32), axis=0),
            jnp.sum(upstream * normed_two, axis=0),
            jnp.sum(upstream, axis=0),
        ),
        ("dp", "tensor"),
    )
    weight_parts = (
        lax.psum_scatter(
            weight_qkv.astype(jnp.bfloat16), "dp", scatter_dimension=1, tiled=True
        ).astype(jnp.float32),
        lax.psum_scatter(
            grad_out.astype(jnp.bfloat16), "dp", scatter_dimension=1, tiled=True
        ).astype(jnp.float32),
        lax.psum_scatter(
            grad_up.astype(jnp.bfloat16), "dp", scatter_dimension=0, tiled=True
        ).astype(jnp.float32),
        lax.psum_scatter(
            grad_down.astype(jnp.bfloat16), "dp", scatter_dimension=1, tiled=True
        ).astype(jnp.float32),
    )
    return (
        result.astype(jnp.bfloat16),
        grad_input,
        weight_parts[0],
        vectors[0],
        vectors[1],
        weight_parts[1],
        vectors[2],
        vectors[3],
        vectors[4],
        weight_parts[2],
        vectors[5],
        weight_parts[3],
        vectors[6],
        vectors[7],
        vectors[8],
    )


def solution(mesh):
    in_specs = (
        P(("dp", "tensor"), None),
        P(("dp", "tensor"), None),
        P(None, None, "tensor"),
        P("tensor"),
        P("tensor"),
        P("tensor", None),
        P(),
        P(),
        P(),
        P(None, "tensor"),
        P("tensor"),
        P("tensor", None),
        P(),
        P(),
        P(),
    )
    out_specs = (
        P(("dp", "tensor"), None),
        P(("dp", "tensor"), None),
        P(None, "dp", "tensor"),
        P(),
        P(),
        P("tensor", "dp"),
        P(),
        P(),
        P(),
        P("dp", "tensor"),
        P(),
        P("tensor", "dp"),
        P(),
        P(),
        P(),
    )
    return jax.shard_map(body, mesh=mesh, in_specs=in_specs, out_specs=out_specs, check_vma=False)
```

profile of v0, /device:TPU:0, one launch (start us, length us, event | category | flops | bytes accessed | tf_op | source)
XLA Modules:
  0.0 1121.9 jit_solution(7841884132667837866)
XLA Ops:
  9.6 59.4 %all-gather.5.cloned.1.call-done = bf16[2048,1024]{1,0:T(8,128)(2,1)} async-done(((bf16[1024,1024]{1,0:T(8,128)(2,1)}), bf16[2048,1024]{1,0:T(8,128)(2,1)}) %all-gather.5.cloned.1.call-update) | async-done | bytes 4194320 | tf_op jit(solution)/shard_map/all_gather | solution.py:87
  69.1 8.8 convolution_bitcast_fusion
  79.5 3.9 fusion.84
  83.4 6.0 squeeze.33
  89.4 4.5 convert_element_type.126
  93.9 3.4 copy.72
  97.3 6.0 squeeze.32
  103.3 8.2 fusion.73
  113.0 33.2 %while.26 = (s32[]{:T(128)}, bf16[4,512,8,64]{1,3,2,0:T(8,128)(2,1)}, f32[4,8,512]{2,1,0:T(8,128)}, bf16[4,512,8,64]{1,3,2,0:T(8,128)(2,1)}, bf16[4,512,8,64]{1,...) while((s32[]{:T(128)}, bf16[4,512,8,64]{1,3,2,0:T(8,128)(2,1)}, f32[4,8,512]{2,1,0:T(8,128)}, ...), condition=%wide.region_3.4_spmd, body=%wide.region_0.3_spmd.sunk | while | flops 556003328 | bytes 27396184 | solution.py:95
  117.1 3.7 fusion.129
  125.4 3.7 fusion.129
  133.6 3.7 fusion.129
  141.9 3.7 fusion.129
  146.2 3.3 copy.73
  151.5 5.6 fusion.85
  157.2 99.3 %reduce-scatter.8.cloned.1.call-done = f32[1024,1024]{1,0:T(8,128)} async-done(((f32[2048,1024]{1,0:T(8,128)}), f32[1024,1024]{1,0:T(8,128)}) %reduce-scatter.8.cloned.1.call-update) | async-done | bytes 4194320 | tf_op jit(solution)/shard_map/reduce_scatter | solution.py:98
  256.6 3.5 fusion.83
  264.2 56.9 %all-gather.7.cloned.1.call-done = bf16[2048,1024]{1,0:T(8,128)(2,1)} async-done(((bf16[1024,1024]{1,0:T(8,128)(2,1)}), bf16[2048,1024]{1,0:T(8,128)(2,1)}) %all-gather.7.cloned.1.call-update) | async-done | bytes 4194320 | tf_op jit(solution)/shard_map/all_gather | solution.py:109
  321.1 16.4 %multiply_convert_fusion.1 = (bf16[2048,2048]{1,0:T(8,128)(2,1)S(1)}, f32[2048,2048]{1,0:T(8,128)}) fusion(f32[2048]{0:T(1024)S(1)} %copy-done.27, bf16[2048,1024]{1,0:T(8,128)(2,1)} %all-gather.7.cloned.1.call-done, bf16[1024,2048]{1,0:T(8,128)(2,1)} %param.28), kind=kOutput, calls=%fused_computation.68 | convolution fusion | flops 8615100416 | bytes 33562624 | tf_op jit(solution)/shard_map/dot_general | solution.py:110
  337.5 3.2 copy-done.30
  340.7 10.9 fusion.86
  351.7 99.4 %reduce-scatter.10.cloned.1.call-done = f32[1024,1024]{1,0:T(8,128)} async-done(((f32[2048,1024]{1,0:T(8,128)}), f32[1024,1024]{1,0:T(8,128)}) %reduce-scatter.10.cloned.1.call-update) | async-done | bytes 4194320 | tf_op jit(solution)/shard_map/reduce_scatter | solution.py:114
  451.1 4.3 fusion.82
  458.5 2.9 fusion.69
  461.4 3.1 convert_reduce_fusion.2
  464.5 56.8 %all-gather.9.cloned.1.call-done = bf16[2048,1024]{1,0:T(8,128)(2,1)} async-done(((bf16[1024,1024]{1,0:T(8,128)(2,1)}), bf16[2048,1024]{1,0:T(8,128)(2,1)}) %all-gather.9.cloned.1.call-update) | async-done | bytes 4194320 | tf_op jit(solution)/shard_map/all_gather | solution.py:126
  521.4 21.0 %convert_reduce_fusion = (f32[2048]{0:T(1024)}, bf16[2048,2048]{1,0:T(8,128)(2,1)S(1)}) fusion(f32[2048,2048]{1,0:T(8,128)} %get-tuple-element.257, f32[2048]{0:T(1024)S(1)} %copy-done.27, bf16[2048,1024]{1,0:T(8,128)(2,1)} %all-gather.9.cloned.1.call-done, bf16[2048,1024]{1,0:T(8,128)(2,1)} %param.30), kind=kOutput, calls=%fused_computation.67 | convolution fusion | flops 8644458496 | bytes 33570816 | tf_op jit(solution)/shard_map/td,fd->tf/dot_general | solution.py:129
  542.4 3.2 copy-done.29
  545.6 11.2 fusion.87
  556.8 99.3 %reduce-scatter.12.cloned.1.call-done = f32[1024,1024]{1,0:T(8,128)} async-done(((f32[2048,1024]{1,0:T(8,128)}), f32[1024,1024]{1,0:T(8,128)}) %reduce-scatter.12.cloned.1.call-update) | async-done | bytes 4194320 | tf_op jit(solution)/shard_map/reduce_scatter | solution.py:132
  656.2 8.9 multiply_reduce_fusion.2
  665.1 4.1 convert_reduce_fusion.3
  669.3 14.1 %convolution_convert_fusion.1 = bf16[2048,1024]{0,1:T(8,128)(2,1)} fusion(bf16[2048,2048]{1,0:T(8,128)(2,1)} %copy-done.30, bf16[2048,1024]{1,0:T(8,128)(2,1)} %all-gather.9.cloned.1.call-done), kind=kOutput, calls=%fused_computation.107 | convolution fusion | flops 8592031744 | bytes 16777216 | tf_op jit(solution)/shard_map/tf,td->fd/dot_general | solution.py:127
  683.5 14.0 %convolution_convert_fusion = bf16[1024,2048]{1,0:T(8,128)(2,1)} fusion(bf16[2048,1024]{1,0:T(8,128)(2,1)} %all-gather.7.cloned.1.call-done, bf16[2048,2048]{1,0:T(8,128)(2,1)} %copy-done.29), kind=kOutput, calls=%fused_computation.106 | convolution fusion | flops 8592031744 | bytes 16777216 | tf_op jit(solution)/shard_map/td,tf->df/dot_general | solution.py:131
  697.6 28.5 %all-gather.11.cloned.1.call-done = bf16[2048,1024]{1,0:T(8,128)(2,1)} async-done(((bf16[1024,1024]{1,0:T(8,128)(2,1)}), bf16[2048,1024]{1,0:T(8,128)(2,1)}) %all-gather.11.cloned.1.call-update) | async-done | bytes 4194320 | tf_op jit(solution)/shard_map/all_gather | solution.py:140
  726.1 6.2 convolution_convert_fusion.2
  732.4 6.4 reshape.134
  738.8 5.6 copy.76
  749.0 69.8 %while.27 = (s32[]{:T(128)}, bf16[4,512,8,64]{1,3,2,0:T(8,128)(2,1)}, bf16[4,512,8,64]{1,3,2,0:T(8,128)(2,1)}, bf16[4,512,8,64]{1,3,2,0:T(8,128)(2,1)}, bf16[4,5...) while((s32[]{:T(128)}, ...), condition=%wide.region_17.18_spmd, body=%wide.region_15.17_spmd.sunk | while | flops 1368649728 | bytes 76665992 | solution.py:145
  754.8 3.2 multiply_reduce_fusion.10
  760.6 3.2 fusion.140
  772.2 3.2 multiply_reduce_fusion.10
  778.0 3.3 fusion.140
  781.3 2.7 fusion.139
  789.7 3.2 multiply_reduce_fusion.10
  795.5 3.2 fusion.140
  807.1 3.2 multiply_reduce_fusion.10
  812.9 3.3 fusion.140
  816.2 2.7 fusion.139
  818.9 5.7 copy.94
  824.6 6.5 reshape.135
  831.1 5.7 copy.96
  836.8 6.5 reshape.137
  843.3 5.7 copy.95
  848.9 6.7 reshape.136
  861.3 8.2 convert_bitcast_fusion
  869.6 7.6 copy.84
  877.3 6.2 convolution_convert_fusion.3
  883.6 11.1 bitcast_convert_fusion
  905.1 41.4 %all-reduce.1 = (f32[1024]{0:T(1024)}, f32[1024]{0:T(1024)}, f32[1024]{0:T(1024)}, f32[1024]{0:T(1024)}, f32[1024]{0:T(1024)}, /*index=5*/f32[4096]{0:T(1024)}, f32[1024]{0:T(1024)}, f32[1024]{0:T(1024)}, f32[1024]{0:T(1024)}) all-reduce(f32[1024]{0:T(1024)S(1)} %dynamic_update_slice.26, ...), channel_id=1, replica_groups=mesh['dp'=16,'tensor'=2] {'dp','tensor'}, use_global_device_ids=true, to_apply=%region_21.22 | all-reduce | flops 12288 | bytes 98304 | tf_op jit(solution)/shard_map/psum | solution.py:172
  946.4 46.7 %all-reduce.4.cloned.1.call-done = bf16[3,1024,512]{2,0,1:T(4,128)(2,1)} async-done(((bf16[3,1024,512]{2,0,1:T(4,128)(2,1)}), bf16[3,1024,512]{2,0,1:T(4,128)(2,1)}) %all-reduce.4.cloned.1.call-update) | async-done | bytes 3145744
  995.0 58.1 %reduce-scatter.16.cloned.1.call-done = bf16[512,64]{0,1:T(8,128)(2,1)} async-done(((bf16[512,1024]{0,1:T(8,128)(2,1)}), bf16[512,64]{0,1:T(8,128)(2,1)}) %reduce-scatter.16.cloned.1.call-update) | async-done | bytes 65552 | tf_op jit(solution)/shard_map/reduce_scatter | solution.py:190
  1054.6 54.1 %reduce-scatter.14.cloned.1.call-done = bf16[1024,1024]{1,0:T(8,128)(2,1)} async-done(((bf16[2048,1024]{1,0:T(8,128)(2,1)}), bf16[1024,1024]{1,0:T(8,128)(2,1)}) %reduce-scatter.14.cloned.1.call-update) | async-done | bytes 2097168 | tf_op jit(solution)/shard_map/reduce_scatter | solution.py:158
  1108.6 5.9 convert_add_fusion
  (161 shorter events, 95.3 us)
Async XLA Ops:
  7.2 61.9 %copy-start = (bf16[3,1024,512]{2,1,0:T(8,128)(2,1)S(1)}, bf16[3,1024,512]{2,1,0:T(8,128)(2,1)}, u32[]{:S(2)}) copy-start(bf16[3,1024,512]{2,1,0:T(8,128)(2,1)} %param.21) | copy-start | bytes 9437188
  7.2 61.9 %all-gather.5.cloned.1.call-start = ((), (), s32[]{:S(2)}) async-start(), calls=%async_computation.7 | async-start | bytes 6291456 | tf_op jit(solution)/shard_map/all_gather | solution.py:87
  7.9 248.6 %reduce-scatter.8.cloned.1.call-start = ((), (), s32[]{:S(2)}) async-start(), calls=%async_computation.8 | async-start | bytes 12582912 | tf_op jit(solution)/shard_map/reduce_scatter | solution.py:98
  146.2 5.3 copy-start.26
  150.2 1.4 copy-start.8
  157.2 99.4 %copy-start.20 = (f32[1024]{0:T(1024)S(1)}, f32[1024]{0:T(1024)}, u32[]{:S(2)}) copy-start(f32[1024]{0:T(1024)} %param.25) | copy-start | bytes 12292
  157.2 163.9 %all-gather.7.cloned.1.call-start = ((), (), s32[]{:S(2)}) async-start(), calls=%async_computation.9 | async-start | bytes 6291456 | tf_op jit(solution)/shard_map/all_gather | solution.py:109
  260.1 2.0 copy-start.1
  260.1 2.0 copy-start.10
  260.1 2.0 copy-start.13
  262.1 59.0 %copy-start.27 = (f32[2048]{0:T(1024)S(1)}, f32[2048]{0:T(1024)}, u32[]{:S(2)}) copy-start(f32[2048]{0:T(1024)} %param.29) | copy-start | bytes 24580
  264.2 186.9 %reduce-scatter.10.cloned.1.call-start = ((), (), s32[]{:S(2)}) async-start(), calls=%async_computation.10 | async-start | bytes 12582912 | tf_op jit(solution)/shard_map/reduce_scatter | solution.py:114
  321.1 19.6 %copy-start.23 = (bf16[2048,1024]{1,0:T(8,128)(2,1)S(1)}, bf16[2048,1024]{1,0:T(8,128)(2,1)}, u32[]{:S(2)}) copy-start(bf16[2048,1024]{1,0:T(8,128)(2,1)} %param.30) | copy-start | bytes 12582916
  337.5 3.2 copy-start.30
  351.6 99.4 %copy-start.21 = (f32[1024]{0:T(1024)S(1)}, f32[1024]{0:T(1024)}, u32[]{:S(2)}) copy-start(f32[1024]{0:T(1024)} %param.31) | copy-start | bytes 12292
  351.7 169.7 %all-gather.9.cloned.1.call-start = ((), (), s32[]{:S(2)}) async-start(), calls=%async_computation.11 | async-start | bytes 6291456 | tf_op jit(solution)/shard_map/all_gather | solution.py:126
  455.4 6.0 copy-start.3
  455.4 3.1 copy-start.5
  455.4 3.1 copy-start.11
  464.5 191.7 %reduce-scatter.12.cloned.1.call-start = ((), (), s32[]{:S(2)}) async-start(), calls=%async_computation.12 | async-start | bytes 12582912 | tf_op jit(solution)/shard_map/reduce_scatter | solution.py:132
  521.4 24.3 %copy-start.24 = (bf16[1024,2048]{1,0:T(8,128)(2,1)S(1)}, bf16[1024,2048]{1,0:T(8,128)(2,1)}, u32[]{:S(2)}) copy-start(bf16[1024,2048]{1,0:T(8,128)(2,1)} %param.28) | copy-start | bytes 12582916
  542.4 3.2 copy-start.29
  556.8 99.4 %copy-start.22 = (f32[1024]{0:T(1024)S(1)}, f32[1024]{0:T(1024)}, u32[]{:S(2)}) copy-start(f32[1024]{0:T(1024)} %param.33) | copy-start | bytes 12292
  556.8 169.3 %all-gather.11.cloned.1.call-start = ((), (), s32[]{:S(2)}) async-start(), calls=%async_computation.13 | async-start | bytes 6291456 | tf_op jit(solution)/shard_map/all_gather | solution.py:140
  656.2 8.9 copy-start.2
  669.2 227.7 %reduce-scatter.20.cloned.1.call-start = ((), (), s32[]{:S(2)}) async-start(), calls=%async_computation.17 | async-start | bytes 4456448 | tf_op jit(solution)/shard_map/reduce_scatter | solution.py:196
  683.4 215.3 %reduce-scatter.18.cloned.1.call-start = ((), (), s32[]{:S(2)}) async-start(), calls=%async_computation.16 | async-start | bytes 4456448 | tf_op jit(solution)/shard_map/reduce_scatter | solution.py:193
  697.5 295.6 %all-reduce.4.cloned.1.call-start = ((), (), s32[]{:S(2)}) async-start(), calls=%async_computation.18 | async-start | bytes 8388608
  749.8 2.7 copy-start.4
  767.2 2.6 copy-start.4
  784.7 2.6 copy-start.4
  802.1 2.7 copy-start.4
  855.6 2.2 copy-start.7
  855.6 2.9 copy-start.6
  857.9 3.5 copy-start.25
  858.7 2.7 copy-start.9
  877.2 175.8 %reduce-scatter.16.cloned.1.call-start = ((), (), s32[]{:S(2)}) async-start(), calls=%async_computation.15 | async-start | bytes 1114112 | tf_op jit(solution)/shard_map/reduce_scatter | solution.py:190
  883.5 225.1 %reduce-scatter.14.cloned.1.call-start = ((), (), s32[]{:S(2)}) async-start(), calls=%async_computation.14 | async-start | bytes 6291456 | tf_op jit(solution)/shard_map/reduce_scatter | solution.py:158
  894.7 0.7 copy-start.28
  894.7 1.9 copy-start.19
  894.7 10.3 copy-start.12
  894.7 10.3 copy-start.14
  894.7 10.3 copy-start.15
  894.7 10.3 copy-start.16
  894.7 10.3 copy-start.17
  894.7 10.3 copy-start.18
Sparse Core Ops, SparseCore 0:
  9.6 59.4 all-gather.4
  157.3 99.2 reduce-scatter.7
  264.3 56.7 all-gather.6
  351.8 99.2 reduce-scatter.9
  464.6 56.7 all-gather.8
  556.9 99.2 reduce-scatter.11
  669.3 56.7 all-gather.10
  730.5 72.3 reduce-scatter.19
  806.7 71.5 reduce-scatter.17
  882.3 110.7 all-reduce.3
  996.7 56.2 reduce-scatter.15
  1055.3 53.2 reduce-scatter.13
where the time goes:
time: 1130 us; the launch traced here: 1120 us
  waiting for transfers between devices  659 us (58%)
  matrix products  215 us (19%)
  local copies, waits for them, and re-layouts  117 us (10%)
  other arithmetic  72.4 us (6%)
  blocking collectives  41.4 us (4%)
  between operations  15.6 us (1%)
    reduce_scatter x1, waiting for transfers between devices, body(): lax.psum_scatter(jnp.dot(active_low, w_down, preferred_element_type=jnp.f...  99.4 us
    reduce_scatter x1, waiting for transfers between devices, body(): lax.psum_scatter(jnp.dot(context, w_out, preferred_element_type=jnp.float...  99.3 us
    reduce_scatter x1, waiting for transfers between devices, body(): lax.psum_scatter(jnp.einsum('tf,df->td', grad_inner, w_up, preferred_elem...  99.3 us
    all_gather x1, waiting for transfers between devices, body(): full_rows = lax.all_gather(tokens, 'tensor', axis=0, tiled=True)  59.4 us
    reduce_scatter x1, waiting for transfers between devices, body(): lax.psum_scatter(grad_out.astype(jnp.bfloat16), 'dp', scatter_dimension=1...  58.1 us
    all_gather x1, waiting for transfers between devices, body(): lax.all_gather(hidden_one.astype(jnp.bfloat16), 'tensor', axis=0, tiled=T...  56.9 us
    all_gather x1, waiting for transfers between devices, body(): branch_rows = lax.all_gather(grad_branch, 'tensor', axis=0, tiled=True)  56.8 us
    reduce_scatter x1, waiting for transfers between devices, body(): lax.psum_scatter(jnp.einsum('kte,kde->td', grad_stack, w_qkv, preferred_e...  54.1 us
  transfers between devices with their start and end apart: 12, of which 10 were waited for; matrix products, arithmetic and copies ran while one was open for 18% of the time, Pallas kernels for 0%

commit v1 on v0

--- a/solution.py
+++ b/solution.py
@@ -1,6 +1,10 @@
+import functools
+
 import jax
 import jax.numpy as jnp
 from jax import lax
+from jax.experimental import pallas as pl
+from jax.experimental.pallas import tpu as pltpu
 from jax.sharding import PartitionSpec as P
 
 D = 1024
@@ -66,7 +70,7 @@
     return (grad_q.astype(jnp.bfloat16), grad_k.astype(jnp.bfloat16), grad_v.astype(jnp.bfloat16))
 
 
-def body(
+def body_tensor(
     tokens,
     cotangent,
     w_qkv,
@@ -216,6 +220,389 @@
     )
 
 
+AXES = ("dp", "tensor")
+LOG2E = 1.4426950408889634
+VMEM = 56 * 1024 * 1024
+NT = (((1,), (1,)), ((), ()))
+
+
+def dot(left, right):
+    return jnp.dot(left, right, preferred_element_type=jnp.float32)
+
+
+def dot_nt(left, right):
+    return lax.dot_general(left, right, NT, preferred_element_type=jnp.float32)
+
+
+def head_masks(width):
+    lane = lax.broadcasted_iota(jnp.int32, (1, width), 1)
+    return lane < HEAD_DIM
+
+
+def attend_kernel(q_ref, k_ref, v_ref, c_ref, l_ref):
+    width = q_ref.shape[1]
+    first = head_masks(128)
+    for pair in range(width // 128):
+        cols = slice(pair * 128, pair * 128 + 128)
+        queries, key_rows = q_ref[:, cols], k_ref[:, cols]
+        values_t = v_ref[:, cols].T
+        parts = []
+        for head in range(2):
+            mask = first if head == 0 else jnp.logical_not(first)
+            picked = jnp.where(mask, queries, jnp.zeros_like(queries))
+            scores = dot_nt(key_rows, picked) * (LOG2E * HEAD_DIM**-0.5)
+            peak = jnp.max(scores, axis=0, keepdims=True)
+            lifted = jnp.exp2(scores - peak)
+            totals = jnp.sum(lifted, axis=0, keepdims=True)
+            context = dot(
+                values_t[head * HEAD_DIM : (head + 1) * HEAD_DIM], lifted.astype(jnp.bfloat16)
+            )
+            parts.append(context * (1.0 / totals))
+            l_ref[0, pair * 2 + head : pair * 2 + head + 1, :] = peak + jnp.log2(totals)
+        c_ref[:, cols] = jnp.concatenate(parts, axis=0).T.astype(jnp.bfloat16)
+
+
+def attend_forward(queries, key_rows, values):
+    rows, width = queries.shape
+    block = min(width, 512)
+    heads = block // HEAD_DIM
+    seqs, groups = rows // SEQ, width // block
+    spec = pl.BlockSpec((SEQ, block), lambda s, g: (s, g))
+    return pl.pallas_call(
+        attend_kernel,
+        grid=(seqs, groups),
+        in_specs=[spec] * 3,
+        out_specs=[spec, pl.BlockSpec((1, heads, SEQ), lambda s, g: (s * groups + g, 0, 0))],
+        out_shape=[
+            jax.ShapeDtypeStruct((rows, width), jnp.bfloat16),
+            jax.ShapeDtypeStruct((seqs * groups, heads, SEQ), jnp.float32),
+        ],
+        compiler_params=pltpu.CompilerParams(vmem_limit_bytes=VMEM),
+        cost_estimate=pl.CostEstimate(
+            flops=rows * width * SEQ * 4, bytes_accessed=rows * width * 8, transcendentals=rows * SEQ * width // HEAD_DIM
+        ),
+        name="attend_forward",
+    )(queries, key_rows, values)
+
+
+def attend_back_kernel(q_ref, k_ref, v_ref, l_ref, dc_ref, d_ref):
+    width = q_ref.shape[1]
+    scale = HEAD_DIM**-0.5
+    first = head_masks(128)
+    for pair in range(width // 128):
+        cols = slice(pair * 128, pair * 128 + 128)
+        queries, key_rows, values = q_ref[:, cols], k_ref[:, cols], v_ref[:, cols]
+        grad_ctx = dc_ref[:, cols]
+        keys_t = key_rows.T
+        parts = []
+        grad_k = grad_v = None
+        for head in range(2):
+            mask = first if head == 0 else jnp.logical_not(first)
+            picked = jnp.where(mask, queries, jnp.zeros_like(queries))
+            grad_picked = jnp.where(mask, grad_ctx, jnp.zeros_like(grad_ctx))
+            level = l_ref[0, pair * 2 + head : pair * 2 + head + 1, :]
+            weights = jnp.exp2(dot_nt(key_rows, picked) * (LOG2E * scale) - level)
+            grad_weights = dot_nt(values, grad_picked)
+            rowsum = jnp.sum(weights * grad_weights, axis=0, keepdims=True)
+            grad_low = (weights * (grad_weights - rowsum)).astype(jnp.bfloat16)
+            piece_v = dot(weights.astype(jnp.bfloat16), grad_picked)
+            piece_k = dot(grad_low, picked)
+            grad_v = piece_v if grad_v is None else grad_v + piece_v
+            grad_k = piece_k if grad_k is None else grad_k + piece_k
+            parts.append(dot(keys_t[head * HEAD_DIM : (head + 1) * HEAD_DIM], grad_low))
+        grad_q = jnp.concatenate(parts, axis=0).T
+        d_ref[0, :, cols] = (grad_q * scale).astype(jnp.bfloat16)
+        d_ref[1, :, cols] = (grad_k * scale).astype(jnp.bfloat16)
+        d_ref[2, :, cols] = grad_v.astype(jnp.bfloat16)
+
+
+def attend_backward(queries, key_rows, values, level, grad_ctx):
+    rows, width = queries.shape
+    block = min(width, 512)
+    heads = block // HEAD_DIM
+    seqs, groups = rows // SEQ, width // block
+    spec = pl.BlockSpec((SEQ, block), lambda s, g: (s, g))
+    return pl.pallas_call(
+        attend_back_kernel,
+        grid=(seqs, groups),
+        in_specs=[spec] * 3
+        + [pl.BlockSpec((1, heads, SEQ), lambda s, g: (s * groups + g, 0, 0)), spec],
+        out_specs=pl.BlockSpec((3, SEQ, block), lambda s, g: (0, s, g)),
+        out_shape=jax.ShapeDtypeStruct((3, rows, width), jnp.bfloat16),
+        compiler_params=pltpu.CompilerParams(vmem_limit_bytes=VMEM),
+        cost_estimate=pl.CostEstimate(
+            flops=rows * width * SEQ * 10, bytes_accessed=rows * width * 14, transcendentals=rows * SEQ * width // HEAD_DIM
+        ),
+        name="attend_backward",
+    )(queries, key_rows, values, level, grad_ctx)
+
+
+def weight_grad_kernel(me_ref, a_ref, by_own, bx_own, by_oth, bx_oth, keep_y, send_y, keep_x, send_x, turned):
+    rel, step = pl.program_id(0), pl.program_id(1)
+    pieces = 16
+    height = turned.shape[0] // pieces
+
+    @pl.when(jnp.logical_and(rel == 0, step == 0))
+    def _():
+        whole = a_ref[...].T
+        me = me_ref[0]
+        for piece in range(pieces):
+            same = (me ^ piece) ^ 15
+            spot = (same & 1) * 8 + (same & 2) * 2 + (same & 4) // 2 + (same & 8) // 8
+            turned[pl.ds(pl.multiple_of(spot * height, height), height), :] = whole[
+                piece * height : (piece + 1) * height
+            ]
+
+    half = turned.shape[0] // 2
+
+    def work(y_ref, x_ref):
+        for src, keep, send in ((y_ref, keep_y, send_y), (x_ref, keep_x, send_x)):
+            right = src[...].reshape(src.shape[-2:])
+            send[...] = dot(turned[:half], right).astype(jnp.bfloat16).reshape(send.shape)
+            keep[...] = dot(turned[half:], right).astype(jnp.bfloat16).reshape(keep.shape)
+
+    @pl.when(rel == 0)
+    def _():
+        work(by_oth, bx_oth)
+
+    @pl.when(rel == 1)
+    def _():
+        work(by_own, bx_own)
+
+
+def weight_grad(place, left, own, other, tile):
+    rows, depth = left.shape
+    stacked = own.ndim == 3
+    if stacked:
+        kinds, _, width = own.shape
+        steps = kinds
+        assert tile * 2 == width
+        shape = (1, rows, tile)
+        y_map, x_map = (lambda j: (j, 0, 0)), (lambda j: (j, 0, 1))
+        columns = kinds * width // 2
+    else:
+        width = own.shape[1]
+        steps = width // 2 // tile
+        shape = (rows, tile)
+        y_map, x_map = (lambda j: (0, j)), (lambda j: (0, j + steps))
+        columns = width // 2
+    height = depth // 16
+
+    def own_map(index_map):
+        return lambda r, j, me: index_map(j * r)
+
+    def other_map(index_map):
+        return lambda r, j, me: index_map(jnp.where(r == 0, j, steps - 1))
+
+    y_shape = jax.ShapeDtypeStruct((2, 2, 2, 2, height, columns), jnp.bfloat16)
+    y_spec = pl.BlockSpec((1, 2, 2, 2, height, tile), lambda r, j, me: (r, 0, 0, 0, 0, j))
+    x_spec = pl.BlockSpec((2, 1, 2, 2, height, tile), lambda r, j, me: (0, r, 0, 0, 0, j))
+    return pl.pallas_call(
+        weight_grad_kernel,
+        grid_spec=pltpu.PrefetchScalarGridSpec(
+            num_scalar_prefetch=1,
+            grid=(2, steps),
+            in_specs=[
+                pl.BlockSpec((rows, depth), lambda r, j, me: (0, 0)),
+                pl.BlockSpec(shape, own_map(y_map)),
+                pl.BlockSpec(shape, own_map(x_map)),
+                pl.BlockSpec(shape, other_map(y_map)),
+                pl.BlockSpec(shape, other_map(x_map)),
+            ],
+            out_specs=[y_spec, y_spec, x_spec, x_spec],
+            scratch_shapes=[pltpu.VMEM((depth, rows), jnp.bfloat16)],
+        ),
+        out_shape=[y_shape] * 4,
+        compiler_params=pltpu.CompilerParams(vmem_limit_bytes=VMEM),
+        cost_estimate=pl.CostEstimate(
+            flops=rows * depth * columns * 8, bytes_accessed=rows * depth * 2 + rows * columns * 8 + depth * columns * 8, transcendentals=0
+        ),
+        name="weight_grad",
+    )(place, left, own, own, other, other)
+
+
+def add_low(*parts):
+    total = parts[0].astype(jnp.float32)
+    for part in parts[1:]:
+        total = total + part.astype(jnp.float32)
+    return total
+
+
+def body(mesh, *args):
+    tokens, w_qkv = args[0], args[2]
+    n_dp, n_tensor = mesh.shape["dp"], mesh.shape["tensor"]
+    if n_dp == 16 and n_tensor == 2 and tokens.shape[0] % SEQ == 0 and w_qkv.shape[2] % 256 == 0:
+        return body_tokens(*args)
+    return body_tensor(*args)
+
+
+def body_tokens(
+    tokens,
+    cotangent,
+    w_qkv,
+    bias_q,
+    bias_v,
+    w_out,
+    bias_o,
+    gain_one,
+    shift_one,
+    w_up,
+    bias_up,
+    w_down,
+    bias_down,
+    gain_two,
+    shift_two,
+):
+    me_dp, me_t = lax.axis_index("dp"), lax.axis_index("tensor")
+    core = me_dp % 2
+    place = me_dp.reshape(1).astype(jnp.int32)
+
+    def swap(value, dp_bit=0, tensor_bit=0):
+        pairs = [
+            ((d * 2 + t), ((d ^ dp_bit) * 2 + (t ^ tensor_bit))) for d in range(16) for t in range(2)
+        ]
+        return lax.ppermute(value, AXES, pairs)
+
+    def other_half(weight, axis):
+        size = weight.shape[axis] // 2
+        mine = lax.dynamic_slice_in_dim(weight, core * size, size, axis)
+        mine = swap(mine, tensor_bit=1)
+        theirs = swap(mine, dp_bit=1)
+        return jnp.where(
+            core == 0,
+            jnp.concatenate([mine, theirs], axis),
+            jnp.concatenate([theirs, mine], axis),
+        )
+
+    widths = (bias_q.shape[0], bias_v.shape[0], bias_up.shape[0])
+    biases = swap(jnp.concatenate([bias_q, bias_v, bias_up]), tensor_bit=1)
+    bias_q2 = biases[: widths[0]]
+    bias_v2 = biases[widths[0] : widths[0] + widths[1]]
+    bias_up2 = biases[widths[0] + widths[1] :]
+    w_qkv2 = other_half(w_qkv, 1)
+    w_out2 = other_half(w_out, 0)
+    w_up2 = other_half(w_up, 0)
+    w_down2 = other_half(w_down, 0)
+
+    halves = ((w_qkv, bias_q, bias_v), (w_qkv2, bias_q2, bias_v2))
+    kept = []
+    for weight, b_q, b_v in halves:
+        queries = (dot(tokens, weight[0]) + b_q).astype(jnp.bfloat16)
+        key_rows = dot(tokens, weight[1]).astype(jnp.bfloat16)
+        values = (dot(tokens, weight[2]) + b_v).astype(jnp.bfloat16)
+        context, level = attend_forward(queries, key_rows, values)
+        kept.append((queries, key_rows, values, level, context))
+    ctx, ctx2 = kept[0][4], kept[1][4]
+    attended = dot(ctx, w_out) + dot(ctx2, w_out2) + bias_o
+    hidden_one, normed_one, scaled_one = norm_forward(
+        tokens.astype(jnp.float32) + attended, gain_one, shift_one
+    )
+    hidden_rows = hidden_one.astype(jnp.bfloat16)
+
+    def expand(weight, bias):
+        activated, slope = gelu_pair(dot(hidden_rows, weight) + bias)
+        return activated.astype(jnp.bfloat16), slope.astype(jnp.bfloat16)
+
+    active, slope = expand(w_up, bias_up)
+    active2, slope2 = expand(w_up2, bias_up2)
+    branch = dot(active, w_down) + dot(active2, w_down2) + bias_down
+    result, normed_two, scaled_two = norm_forward(hidden_one + branch, gain_two, shift_two)
+    upstream = cotangent.astype(jnp.float32)
+    grad_two = norm_backward(upstream, gain_two, normed_two, scaled_two)
+    grad_branch = grad_two.astype(jnp.bfloat16)
+
+    parts_down = weight_grad(place, grad_branch, active, active2, 512)
+    grad_inner = (dot_nt(grad_branch, w_down) * slope.astype(jnp.float32)).astype(jnp.bfloat16)
+    grad_inner2 = (dot_nt(grad_branch, w_down2) * slope2.astype(jnp.float32)).astype(jnp.bfloat16)
+    parts_up = weight_grad(place, hidden_rows, grad_inner, grad_inner2, 512)
+    grad_hidden = grad_two + dot_nt(grad_inner, w_up) + dot_nt(grad_inner2, w_up2)
+    grad_one = norm_backward(grad_hidden, gain_one, normed_one, scaled_one)
+    grad_attended = grad_one.astype(jnp.bfloat16)
+    parts_out = weight_grad(place, grad_attended, ctx, ctx2, 256)
+    grad_stack = attend_backward(*kept[0][:4], dot_nt(grad_attended, w_out).astype(jnp.bfloat16))
+    grad_stack2 = attend_backward(*kept[1][:4], dot_nt(grad_attended, w_out2).astype(jnp.bfloat16))
+    parts_qkv = weight_grad(place, tokens, grad_stack, grad_stack2, 256)
+    grad_input = grad_one
+    for stack, weight in ((grad_stack, w_qkv), (grad_stack2, w_qkv2)):
+        for kind in range(3):
+            grad_input = grad_input + dot_nt(stack[kind], weight[kind])
+
+    def scatter(parts):
+        keep_y, send_y, keep_x, send_x = parts
+        outs = []
+        for keep, send, order in (
+            (keep_y, send_y, ((0, 1), (2, 0), (4, 0), (8, 0))),
+            (keep_x, send_x, ((2, 0), (0, 1), (4, 0), (8, 0))),
+        ):
+            addends = [keep, swap(send, dp_bit=1)]
+            for dp_bit, tensor_bit in order:
+                leaving = add_low(*[a[0] for a in addends]).astype(jnp.bfloat16)
+                arrived = swap(leaving, dp_bit, tensor_bit)
+                addends = [add_low(*[a[1] for a in addends]).astype(jnp.bfloat16), arrived]
+            outs.append(add_low(*addends))
+        return outs
+
+    down_y, down_x = scatter(parts_down)
+    up_y, up_x = scatter(parts_up)
+    out_y, out_x = scatter(parts_out)
+    qkv_y, qkv_x = scatter(parts_qkv)
+    grad_down = jnp.concatenate([down_y, down_x], axis=1).T
+    grad_up = jnp.concatenate([up_y, up_x], axis=1)
+    grad_out = jnp.concatenate([out_y, out_x], axis=1).T
+    rows = qkv_y.shape[0]
+    grad_qkv = jnp.concatenate([qkv_y.reshape(rows, 3, -1), qkv_x.reshape(rows, 3, -1)], axis=2)
+    grad_qkv = jnp.transpose(grad_qkv, (1, 0, 2))
+
+    def whole(own, other):
+        own, other = (jnp.sum(v.astype(jnp.float32), axis=0) for v in (own, other))
+        return jnp.where(
+            me_t == 0, jnp.concatenate([own, other]), jnp.concatenate([other, own])
+        )
+
+    def all_sum(pieces):
+        sizes = [piece.shape[0] for piece in pieces]
+        total = jnp.concatenate(pieces)
+        for dp_bit, tensor_bit in ((1, 0), (0, 1), (2, 0), (4, 0), (8, 0)):
+            total = total + swap(total, dp_bit, tensor_bit)
+        result, at = [], 0
+        for size in sizes:
+            result.append(total[at : at + size])
+            at += size
+        return result
+
+    g_shift_two, g_gain_two, g_bias_down, g_bias_up, g_shift_one, g_gain_one, g_bias_o = all_sum(
+        [
+            jnp.sum(upstream, axis=0),
+            jnp.sum(upstream * normed_two, axis=0),
+            jnp.sum(grad_branch.astype(jnp.float32), axis=0),
+            whole(grad_inner, grad_inner2),
+            jnp.sum(grad_hidden, axis=0),
+            jnp.sum(grad_hidden * normed_one, axis=0),
+            jnp.sum(grad_attended.astype(jnp.float32), axis=0),
+        ]
+    )
+    g_bias_q, g_bias_v = all_sum(
+        [whole(grad_stack[0], grad_stack2[0]), whole(grad_stack[2], grad_stack2[2])]
+    )
+    return (
+        result.astype(jnp.bfloat16),
+        grad_input,
+        grad_qkv,
+        g_bias_q,
+        g_bias_v,
+        grad_out,
+        g_bias_o,
+        g_gain_one,
+        g_shift_one,
+        grad_up,
+        g_bias_up,
+        grad_down,
+        g_bias_down,
+        g_gain_two,
+        g_shift_two,
+    )
+
+
 def solution(mesh):
     in_specs = (
         P(("dp", "tensor"), None),
@@ -251,4 +638,4 @@
         P(),
         P(),
     )
-    return jax.shard_map(body, mesh=mesh, in_specs=in_specs, out_specs=out_specs, check_vma=False)
+    return jax.shard_map(functools.partial(body, mesh), mesh=mesh, in_specs=in_specs, out_specs=out_specs, check_vma=False)

time: 1130 us -> 596 us (0.53)
  waiting for transfers between devices: 659 us -> 215 us
  Pallas kernels: 0 us -> 104 us
  local copies, waits for them, and re-layouts: 117 us -> 19.5 us
  matrix products: 215 us -> 140 us
  starting transfers between devices: 0.49 us -> 65.9 us
  blocking collectives: 41.4 us -> 0 us
  other arithmetic: 72.4 us -> 45.3 us
  between operations: 15.6 us -> 1.92 us
    reduce_scatter x7 -> x0, waiting for transfers between devices: 410 us -> none  [the longest x1 99.4 us: body(): lax.psum_scatter(jnp.dot(active_low, w_down, preferred_element_type=jnp.f...]
    ppermute x0 -> x59, waiting for transfers between devices: none -> 215 us  [swap(): return lax.ppermute(value, AXES, pairs)]
    all_gather x4 -> x0, waiting for transfers between devices: 202 us -> none  [the longest x1 59.4 us: body(): full_rows = lax.all_gather(tokens, 'tensor', axis=0, tiled=True)]
    pallas_call x0 -> x8, Pallas kernels: none -> 104 us  [the longest x4 49.6 us: weight_grad(): pl.pallas_call(weight_grad_kernel, grid_spec=pltpu.PrefetchScalarGridSpec...]
    dot_general x40 -> x24, matrix products: 215 us -> 140 us  [the longest x12 83.2 us: dot_nt(): return lax.dot_general(left, right, NT, preferred_element_type=jnp.float32)]
    ppermute x0 -> x59, starting transfers between devices: none -> 65.9 us  [swap(): return lax.ppermute(value, AXES, pairs)]
    unnamed x13 -> x0, waiting for transfers between devices: 47.5 us -> none
    another operation x13 -> x0, local copies, waits for them, and re-layouts: 43.1 us -> none  [the longest x7 36.9 us: body(): jnp.stack([grad_q.reshape(group_rows, local_width), grad_k.reshape(group_...]
  transfers between devices with their start and end apart: 12 -> 59, of which waited for: 10 -> 25; matrix products, arithmetic and copies ran while one was open for 18% -> 18% of each run, Pallas kernels for 0% -> 6%
where the time goes in v1:
time: 596 us; the launch traced here: 592 us
  waiting for transfers between devices  215 us (36%)
  matrix products  140 us (23%)
  Pallas kernels  104 us (17%)
  starting transfers between devices  65.9 us (11%)
  other arithmetic  45.3 us (8%)
  local copies, waits for them, and re-layouts  19.5 us (3%)
    ppermute x59, waiting for transfers between devices, swap(): return lax.ppermute(value, AXES, pairs)  215 us
    dot_general x12, matrix products, dot_nt(): return lax.dot_general(left, right, NT, preferred_element_type=jnp.float32)  83.2 us
    ppermute x59, starting transfers between devices, swap(): return lax.ppermute(value, AXES, pairs)  65.9 us
    dot_general x12, matrix products, dot(): return jnp.dot(left, right, preferred_element_type=jnp.float32)  57.3 us
    pallas_call x4, Pallas kernels, weight_grad(): pl.pallas_call(weight_grad_kernel, grid_spec=pltpu.PrefetchScalarGridSpec...  49.6 us
    pallas_call x2, Pallas kernels, attend_backward(): pl.pallas_call(attend_back_kernel, grid=(seqs, groups), in_specs=[spec] *...  32.9 us
    pallas_call x2, Pallas kernels, attend_forward(): pl.pallas_call(attend_kernel, grid=(seqs, groups), in_specs=[spec] * 3, o...  21.7 us
    convert_element_type x24, other arithmetic, scatter(): addends = [add_low(*[a[1] for a in addends]).astype(jnp.bfloat16), arrived]  19.4 us
  transfers between devices with their start and end apart: 59, of which 25 were waited for; matrix products, arithmetic and copies ran while one was open for 18% of the time, Pallas kernels for 6%

profile of v1, /device:TPU:0, one launch (start us, length us, event | category | flops | bytes accessed | tf_op | source)
XLA Modules:
  0.0 592.3 jit_solution(9466444265422363312)
XLA Ops:
  0.7 2.7 constant_dynamic-slice_fusion.3
  3.4 3.0 collective-permute-start
  6.4 3.2 constant_dynamic-slice_fusion
  9.6 3.2 constant_dynamic-slice_fusion.1
  17.7 24.2 %collective-permute-done = bf16[3,512,512]{2,1,0:T(8,128)(2,1)} collective-permute-done((bf16[3,512,512]{2,1,0:T(8,128)(2,1)}, bf16[3,512,512]{2,1,0:T(8,128)(2,1)}, u32[]{:S(2)}, u32[]{:S(2)}) %collective-permute-start) | collective-permute-done | bytes 1572896 | tf_op jit(solution)/shard_map/ppermute | solution.py:464
  41.9 3.5 convolution_convert_fusion.3.k_ref
  49.9 10.8 %attend_forward.2 = (bf16[1024,512]{1,0:T(8,128)(2,1)}, f32[2,8,512]{2,1,0:T(8,128)}) custom-call(bf16[1024,512]{1,0:T(8,128)(2,1)} %add_convert_fusion.12.q_ref, bf16[1024,512]{1,0:T(8,128)(2,1)} %convolution_convert_fusion.3.k_ref, bf16[1024,512]{1,0:T(8,128)(2,1)} %add_convert_fusion.11.v_ref), custom_call_target="tpu_custom_call" | custom-call | flops 1073741824 | bytes 4194304 | tf_op jit(solution)/shard_map/attend_forward/pallas_call | solution.py:271
  60.6 4.5 fusion.144
  65.1 66.8 %collective-permute-done.2 = f32[3072]{0:T(1024)S(1)} collective-permute-done((f32[3072]{0:T(1024)S(1)}, f32[3072]{0:T(1024)S(1)}, u32[]{:S(2)}, u32[]{:S(2)}) %collective-permute-start.2) | collective-permute-done | bytes 12320 | tf_op jit(solution)/shard_map/ppermute | solution.py:464
  132.0 10.5 %collective-permute-done.3 = bf16[256,1024]{1,0:T(8,128)(2,1)} collective-permute-done((bf16[256,1024]{1,0:T(8,128)(2,1)}, bf16[256,1024]{1,0:T(8,128)(2,1)}, u32[]{:S(2)}, u32[]{:S(2)}) %collective-permute-start.3) | collective-permute-done | bytes 524320 | tf_op jit(solution)/shard_map/ppermute | solution.py:464
  143.1 3.4 maximum_select_fusion.2
  146.5 2.2 fusion.20.v_ref
  148.7 2.2 fusion.18.k_ref
  153.2 10.9 %attend_forward.3 = (bf16[1024,512]{1,0:T(8,128)(2,1)}, f32[2,8,512]{2,1,0:T(8,128)}) custom-call(bf16[1024,512]{1,0:T(8,128)(2,1)} %fusion.19.q_ref, bf16[1024,512]{1,0:T(8,128)(2,1)} %fusion.18.k_ref, bf16[1024,512]{1,0:T(8,128)(2,1)} %fusion.20.v_ref), custom_call_target="tpu_custom_call" | custom-call | flops 1073741824 | bytes 4194304 | tf_op jit(solution)/shard_map/attend_forward/pallas_call | solution.py:271
  164.2 5.2 fusion.142
  172.2 7.1 %multiply_convert_fusion.3 = (bf16[1024,2048]{1,0:T(8,128)(2,1)S(1)}, f32[1024,2048]{1,0:T(8,128)}) fusion(f32[2048]{0:T(1024)S(1)} %copy-done.36, bf16[1024,1024]{1,0:T(8,128)(2,1)S(1)} %fusion.17.a_ref, bf16[1024,2048]{1,0:T(8,128)(2,1)S(1)} %copy-done.24), kind=kOutput, calls=%fused_computation.18 | convolution fusion | flops 4307550208 | bytes 18882560 | tf_op jit(solution)/shard_map/dot_general | solution.py:230
  179.3 6.0 %fusion.145 = f32[1024,1024]{1,0:T(8,128)} fusion(bf16[1024,2048]{1,0:T(8,128)(2,1)S(1)} %get-tuple-element.148.by_own.bx_own, bf16[2048,1024]{1,0:T(8,128)(2,1)S(1)} %copy-done.23), kind=kOutput, calls=%fused_computation.345 | convolution fusion | flops 4294967296 | bytes 12582912 | tf_op jit(solution)/shard_map/dot_general | solution.py:230
  185.3 9.7 %multiply_convert_fusion.2 = (bf16[1024,2048]{1,0:T(8,128)(2,1)S(1)}, f32[1024,2048]{1,0:T(8,128)}) fusion(f32[2048]{0:T(1024)S(1)} %slice.671, bf16[1024,1024]{1,0:T(8,128)(2,1)S(1)} %fusion.17.a_ref, bf16[512,2048]{1,0:T(8,128)(2,1)} %collective-permute-done.6, bf16[512,2048]{1,0:T(8,128)(2,1)} %collective-permute-done.5, pred[]{:T(512)S(6)} %eq.6), kind=kOutput, calls=%fused_computation.16 | convolution fusion | flops 4326424576 | bytes 18882560 | tf_op jit(solution)/shard_map/dot_general | solution.py:230
  195.1 10.1 %fusion.143 = (f32[1024]{0:T(1024)S(1)}, f32[1024,1024]{1,0:T(8,128)S(1)}) fusion(f32[1024]{0:T(1024)S(1)} %copy-done.42, f32[1024,1024]{1,0:T(8,128)} %fusion.145, bf16[1024,2048]{1,0:T(8,128)(2,1)S(1)} %get-tuple-element.150.by_oth.bx_oth, bf16[1024,1024]{1,0:T(8,128)(2,1)} %collective-permute-done.8, bf16[1024,1024]{1,0:T(8,128)(2,1)} %collective-permute-done.7, ...), kind=kOutput, calls=%fused_computation.343 | convolution fusion | flops 4322229248 | bytes 20996096 | tf_op jit(solution)/shard_map/dot_general | solution.py:230
  205.8 2.5 copy-done.3
  208.3 2.4 fusion.16
  210.8 3.0 convert_reduce_fusion.4
  213.8 11.3 %convert_reduce_fusion.1 = (f32[2048]{0:T(1024)S(1)}, bf16[1024,2048]{1,0:T(8,128)(2,1)}) fusion(f32[1024,2048]{1,0:T(8,128)} %get-tuple-element.149, f32[2048]{0:T(1024)S(1)} %copy-done.36, bf16[1024,1024]{1,0:T(8,128)(2,1)S(1)} %get-tuple-element.86.a_ref, bf16[2048,1024]{1,0:T(8,128)(2,1)S(1)} %copy-done.23), kind=kOutput, calls=%fused_computation.13 | convolution fusion | flops 4326422528 | bytes 18890752 | tf_op jit(solution)/shard_map/dot_general | solution.py:234
  225.0 14.8 %weight_grad.7 = (bf16[2,2,2,2,64,1024]{5,4,3,2,1,0:T(8,128)(2,1)}, bf16[2,2,2,2,64,1024]{5,4,3,2,1,0:T(8,128)(2,1)}, bf16[2,2,2,2,64,1024]{5,4,3,2,1,0:T(8,128)(2,1)}, bf16[2,2,2,2,64,1024]{5,4,3,2,1,0:T(8,128)(2,1)}) custom-call(s32[1]{0:T(128)} %bitcast.15.me_ref, bf16[1024,1024]{1,0:T(8,128)(2,1)} %copy-done.18, bf16[1024,2048]{1,0:T(8,128)(2,1)} %copy-done.43, ...), custom_call_target="tpu_custom_call" | custom-call | flops 8589934592 | bytes 18874368 | tf_op jit(solution)/shard_map/weight_grad/pallas_call | solution.py:400
  239.8 10.1 %fusion.146 = f32[1024,1024]{1,0:T(8,128)} fusion(bf16[1024,2048]{1,0:T(8,128)(2,1)} %get-tuple-element.158.by_own.bx_own, bf16[1024,2048]{1,0:T(8,128)(2,1)} %param.24), kind=kOutput, calls=%fused_computation.346 | convolution fusion | flops 4294967296 | bytes 12582912 | tf_op jit(solution)/shard_map/dot_general | solution.py:234
  250.0 13.6 %convert_reduce_fusion = (f32[2048]{0:T(1024)S(1)}, bf16[1024,2048]{1,0:T(8,128)(2,1)}) fusion(f32[1024,2048]{1,0:T(8,128)} %get-tuple-element.151, f32[2048]{0:T(1024)S(1)} %slice.671, bf16[1024,1024]{1,0:T(8,128)(2,1)S(1)} %copy-done.19, bf16[1024,1024]{1,0:T(8,128)(2,1)} %collective-permute-done.8, bf16[1024,1024]{1,0:T(8,128)(2,1)} %collective-permute-done.7, ...), kind=kOutput, calls=%fused_computation.12 | convolution fusion | flops 4345296896 | bytes 18890752 | tf_op jit(solution)/shard_map/dot_general | solution.py:234
  263.5 15.5 %multiply_reduce_fusion = (f32[1024]{0:T(1024)S(1)}, f32[1024]{0:T(1024)S(1)}, f32[1024]{0:T(1024)S(1)}, f32[1024]{0:T(1024)S(1)}, f32[1024,1024]{1,0:T(8,128)}) fusion(f32[1024,1024]{1,0:T(8,128)S(1)} %get-tuple-element.147, f32[1024]{0:T(1024)S(1)} %add_rsqrt_fusion.1, f32[1024]{0:T(1024)S(1)} %broadcast_multiply_fusion.5, f32[1024]{0:T(1024)S(1)} %copy-done.35, ...), kind=kOutput, calls=%fused_computation.33 | convolution fusion | flops 4333760512 | bytes 27312128 | tf_op jit(solution)/shard_map/dot_general | solution.py:234
  279.0 5.0 convert_reduce_fusion.3
  284.0 7.1 %weight_grad.5 = (bf16[2,2,2,2,64,256]{5,4,3,2,1,0:T(8,128)(2,1)}, bf16[2,2,2,2,64,256]{5,4,3,2,1,0:T(8,128)(2,1)}, bf16[2,2,2,2,64,256]{5,4,3,2,1,0:T(8,128)(2,1)}, bf16[2,2,2,2,64,256]{5,4,3,2,1,0:T(8,128)(2,1)}) custom-call(s32[1]{0:T(128)} %bitcast.15.me_ref, bf16[1024,1024]{1,0:T(8,128)(2,1)} %get-tuple-element.83.a_ref, ...), custom_call_target="tpu_custom_call" | custom-call | flops 2147483648 | bytes 6291456 | tf_op jit(solution)/shard_map/weight_grad/pallas_call | solution.py:400
  291.1 2.3 convolution_convert_fusion.2.dc_ref
  293.4 16.6 %attend_backward.2.by_own.bx_own = bf16[3,1024,512]{2,1,0:T(8,128)(2,1)} custom-call(bf16[1024,512]{1,0:T(8,128)(2,1)} %add_convert_fusion.12.q_ref, bf16[1024,512]{1,0:T(8,128)(2,1)} %convolution_convert_fusion.3.k_ref, bf16[1024,512]{1,0:T(8,128)(2,1)} %add_convert_fusion.11.v_ref, f32[2,8,512]{2,1,0:T(8,128)} %get-tuple-element.37.l_ref, ...), custom_call_target="tpu_custom_call" | custom-call | flops 2684354560 | bytes 7340032 | tf_op jit(solution)/shard_map/attend_backward/pallas_call | solution.py:325
  312.0 4.6 fusion.35
  316.6 3.3 fusion.26
  319.9 3.3 fusion.40
  323.3 3.5 convolution_convert_fusion.1.dc_ref
  326.7 16.3 %attend_backward.3.by_oth.bx_oth = bf16[3,1024,512]{2,1,0:T(8,128)(2,1)} custom-call(bf16[1024,512]{1,0:T(8,128)(2,1)} %fusion.19.q_ref, bf16[1024,512]{1,0:T(8,128)(2,1)} %fusion.18.k_ref, bf16[1024,512]{1,0:T(8,128)(2,1)} %fusion.20.v_ref, f32[2,8,512]{2,1,0:T(8,128)} %get-tuple-element.38.l_ref, bf16[1024,512]{1,0:T(8,128)(2,1)} %convolution_convert_fusion.1.dc_ref), custom_call_target="tpu_custom_call" | custom-call | flops 2684354560 | bytes 7340032 | tf_op jit(solution)/shard_map/attend_backward/pallas_call | solution.py:325
  344.9 12.8 %weight_grad.4 = (bf16[2,2,2,2,64,768]{5,4,3,2,1,0:T(8,128)(2,1)}, bf16[2,2,2,2,64,768]{5,4,3,2,1,0:T(8,128)(2,1)}, bf16[2,2,2,2,64,768]{5,4,3,2,1,0:T(8,128)(2,1)}, bf16[2,2,2,2,64,768]{5,4,3,2,1,0:T(8,128)(2,1)}) custom-call(s32[1]{0:T(128)} %bitcast.15.me_ref, bf16[1024,1024]{1,0:T(8,128)(2,1)} %a_ref.1, ...), custom_call_target="tpu_custom_call" | custom-call | flops 6442450944 | bytes 14680064 | tf_op jit(solution)/shard_map/weight_grad/pallas_call | solution.py:400
  361.3 3.3 fusion.25
  366.9 3.4 fusion.43
  376.0 9.0 %add_add_fusion = f32[1024,1024]{1,0:T(8,128)} fusion(f32[1024,1024]{1,0:T(8,128)} %fusion.25, f32[1024,1024]{1,0:T(8,128)} %fusion.43, f32[1024,1024]{1,0:T(8,128)S(1)} %copy-done.7, f32[1024,1024]{1,0:T(8,128)S(1)} %copy-done.8, f32[1024,1024]{1,0:T(8,128)S(1)} %copy-done.2, f32[1024,1024]{1,0:T(8,128)} %fusion.40, ...), kind=kOutput, calls=%fused_computation.35 | convolution fusion | flops 1080033280 | bytes 31457280 | tf_op jit(solution)/shard_map/dot_general | solution.py:234
  385.0 2.7 collective-permute-start.23
  388.9 4.6 collective-permute-done.26
  394.1 4.4 collective-permute-done.31
  400.1 3.3 collective-permute-done.27
  405.1 3.0 collective-permute-done.32
  408.1 2.2 collective-permute-start.28
  412.9 2.2 collective-permute-start.33
  415.1 15.0 %weight_grad.6 = (bf16[2,2,2,2,64,1024]{5,4,3,2,1,0:T(8,128)(2,1)}, bf16[2,2,2,2,64,1024]{5,4,3,2,1,0:T(8,128)(2,1)}, bf16[2,2,2,2,64,1024]{5,4,3,2,1,0:T(8,128)(2,1)}, bf16[2,2,2,2,64,1024]{5,4,3,2,1,0:T(8,128)(2,1)}) custom-call(s32[1]{0:T(128)} %bitcast.15.me_ref, bf16[1024,1024]{1,0:T(8,128)(2,1)} %copy-done.14, ...), custom_call_target="tpu_custom_call" | custom-call | flops 8589934592 | bytes 18874368 | tf_op jit(solution)/shard_map/weight_grad/pallas_call | solution.py:400
  435.5 3.6 add_convert_fusion.4
  440.6 2.3 add_convert_fusion.2
  446.3 8.0 %collective-permute-done.10 = bf16[2,2,2,64,768]{4,3,2,1,0:T(8,128)(2,1)S(1)} collective-permute-done((bf16[2,2,2,64,768]{4,3,2,1,0:T(8,128)(2,1)S(1)}, bf16[2,2,2,64,768]{4,3,2,1,0:T(8,128)(2,1)S(1)}, u32[]{:S(2)}, u32[]{:S(2)}) %collective-permute-start.10) | collective-permute-done | bytes 786464 | tf_op jit(solution)/shard_map/ppermute | solution.py:464
  457.8 2.3 add_convert_fusion.6
  460.1 24.9 %collective-permute-done.11 = bf16[2,2,64,768]{3,2,1,0:T(8,128)(2,1)S(1)} collective-permute-done((bf16[2,2,64,768]{3,2,1,0:T(8,128)(2,1)S(1)}, bf16[2,2,64,768]{3,2,1,0:T(8,128)(2,1)S(1)}, u32[]{:S(2)}, u32[]{:S(2)}) %collective-permute-start.11) | collective-permute-done | bytes 393248 | tf_op jit(solution)/shard_map/ppermute | solution.py:464
  485.7 21.0 %collective-permute-done.16 = bf16[2,2,64,768]{3,2,1,0:T(8,128)(2,1)S(1)} collective-permute-done((bf16[2,2,64,768]{3,2,1,0:T(8,128)(2,1)S(1)}, bf16[2,2,64,768]{3,2,1,0:T(8,128)(2,1)S(1)}, u32[]{:S(2)}, u32[]{:S(2)}) %collective-permute-start.16) | collective-permute-done | bytes 393248 | tf_op jit(solution)/shard_map/ppermute | solution.py:464
  506.7 2.6 collective-permute-start.12
  509.4 4.2 collective-permute-done.12
  515.4 4.2 collective-permute-done.17
  519.6 5.5 collective-permute-done.13
  526.9 3.9 collective-permute-done.18
  547.0 5.8 collective-permute-done.51
  557.1 3.9 collective-permute-done.41
  564.9 9.2 %collective-permute-start.58 = (bf16[64,1024]{1,0:T(8,128)(2,1)S(1)}, bf16[64,1024]{1,0:T(8,128)(2,1)S(1)}, u32[]{:S(2)}, u32[]{:S(2)}) collective-permute-start(bf16[64,1024]{1,0:T(8,128)(2,1)S(1)} %fusion.110), channel_id=1, source_target_pairs={{0,16},{1,17},{2,18},{3,19},{4,20},{5,21},{6,22},{7,23},{8,24},{9,... | collective-permute-start | bytes 393224 | tf_op jit(solution)/shard_map/ppermute | solution.py:464
  574.1 3.3 collective-permute-start.43
  580.4 7.0 %collective-permute-done.58 = bf16[64,1024]{1,0:T(8,128)(2,1)S(1)} collective-permute-done((bf16[64,1024]{1,0:T(8,128)(2,1)S(1)}, bf16[64,1024]{1,0:T(8,128)(2,1)S(1)}, u32[]{:S(2)}, u32[]{:S(2)}) %collective-permute-start.58) | collective-permute-done | bytes 131104 | tf_op jit(solution)/shard_map/ppermute | solution.py:464
  (269 shorter events, 88.1 us)
Async XLA Ops:
  3.4 38.5 %collective-permute-start = (bf16[3,512,512]{2,1,0:T(8,128)(2,1)}, bf16[3,512,512]{2,1,0:T(8,128)(2,1)}, u32[]{:S(2)}, u32[]{:S(2)}) collective-permute-start(bf16[3,512,512]{2,1,0:T(8,128)(2,1)} %constant_dynamic-slice_fusion.3), channel_id=1, source_target_pairs={{0,1},{1,0},{2,3},{3,2},{4,5},{5,4},{6,7},{7,6},{8,9},{9,8},{10,11... | collective-permute-start | bytes 4718600 | tf_op jit(solution)/shard_map/ppermute | solution.py:464
  6.4 35.5 %copy-start.6 = (bf16[1024,1024]{1,0:T(8,128)(2,1)S(1)}, bf16[1024,1024]{1,0:T(8,128)(2,1)}, u32[]{:S(2)}) copy-start(bf16[1024,1024]{1,0:T(8,128)(2,1)} %a_ref.1) | copy-start | bytes 6291460
  9.6 132.9 %collective-permute-start.7 = (bf16[1024,1024]{1,0:T(8,128)(2,1)}, bf16[1024,1024]{1,0:T(8,128)(2,1)}, u32[]{:S(2)}, u32[]{:S(2)}) collective-permute-start(bf16[1024,1024]{1,0:T(8,128)(2,1)} %constant_dynamic-slice_fusion), channel_id=1, source_target_pairs={{0,1},{1,0},{2,3},{3,2},{4,5},{5,4},{6,7},{7,6},{8,9},{9,8},{10,11... | collective-permute-start | bytes 6291464 | tf_op jit(solution)/shard_map/ppermute | solution.py:464
  12.8 130.2 %collective-permute-start.5 = (bf16[512,2048]{1,0:T(8,128)(2,1)}, bf16[512,2048]{1,0:T(8,128)(2,1)}, u32[]{:S(2)}, u32[]{:S(2)}) collective-permute-start(bf16[512,2048]{1,0:T(8,128)(2,1)} %constant_dynamic-slice_fusion.1), channel_id=1, source_target_pairs={{0,1},{1,0},{2,3},{3,2},{4,5},{5,4},{6,7},{7,6},{8,9},{9,8},{10,11... | collective-permute-start | bytes 6291464 | tf_op jit(solution)/shard_map/ppermute | solution.py:464
  14.8 117.1 %collective-permute-start.2 = (f32[3072]{0:T(1024)S(1)}, f32[3072]{0:T(1024)S(1)}, u32[]{:S(2)}, u32[]{:S(2)}) collective-permute-start(f32[3072]{0:T(1024)S(1)} %pad_maximum_fusion.1), channel_id=1, source_target_pairs={{0,1},{1,0},{2,3},{3,2},{4,5},{5,4},{6,7},{7,6},{8,9},{9,8},{10,11... | collective-permute-start | bytes 36872 | tf_op jit(solution)/shard_map/ppermute | solution.py:464
  15.8 29.7 %copy-start.26 = (bf16[3,1024,512]{2,1,0:T(8,128)(2,1)S(1)}, bf16[3,1024,512]{2,1,0:T(8,128)(2,1)}, u32[]{:S(2)}) copy-start(bf16[3,1024,512]{2,1,0:T(8,128)(2,1)} %param.17) | copy-start | bytes 9437188
  15.8 126.7 %collective-permute-start.3 = (bf16[256,1024]{1,0:T(8,128)(2,1)}, bf16[256,1024]{1,0:T(8,128)(2,1)}, u32[]{:S(2)}, u32[]{:S(2)}) collective-permute-start(bf16[256,1024]{1,0:T(8,128)(2,1)} %constant_dynamic-slice_fusion.2), channel_id=1, source_target_pairs={{0,1},{1,0},{2,3},{3,2},{4,5},{5,4},{6,7},{7,6},{8,9},{9,8},{10,11... | collective-permute-start | bytes 1572872 | tf_op jit(solution)/shard_map/ppermute | solution.py:464
  41.9 101.1 %collective-permute-start.1 = (bf16[3,512,512]{2,1,0:T(8,128)(2,1)}, bf16[3,512,512]{2,1,0:T(8,128)(2,1)}, u32[]{:S(2)}, u32[]{:S(2)}) collective-permute-start(bf16[3,512,512]{2,1,0:T(8,128)(2,1)} %collective-permute-done), channel_id=1, source_target_pairs={{0,2},{1,3},{2,0},{3,1},{4,6},{5,7},{6,4},{7,5},{8,10},{9,11},{10,... | collective-permute-start | bytes 4718600 | tf_op jit(solution)/shard_map/ppermute | solution.py:464
  142.5 21.7 %collective-permute-start.4 = (bf16[256,1024]{1,0:T(8,128)(2,1)}, bf16[256,1024]{1,0:T(8,128)(2,1)S(1)}, u32[]{:S(2)}, u32[]{:S(2)}) collective-permute-start(bf16[256,1024]{1,0:T(8,128)(2,1)} %collective-permute-done.3), channel_id=1, source_target_pairs={{0,2},{1,3},{2,0},{3,1},{4,6},{5,7},{6,4},{7,5},{8,10},{9,11},{10,... | collective-permute-start | bytes 1572872 | tf_op jit(solution)/shard_map/ppermute | solution.py:464
  142.5 52.6 %collective-permute-start.8 = (bf16[1024,1024]{1,0:T(8,128)(2,1)}, bf16[1024,1024]{1,0:T(8,128)(2,1)}, u32[]{:S(2)}, u32[]{:S(2)}) collective-permute-start(bf16[1024,1024]{1,0:T(8,128)(2,1)} %collective-permute-done.7), channel_id=1, source_target_pairs={{0,2},{1,3},{2,0},{3,1},{4,6},{5,7},{6,4},{7,5},{8,10},{9,11},{10,... | collective-permute-start | bytes 6291464 | tf_op jit(solution)/shard_map/ppermute | solution.py:464
  143.0 42.3 %collective-permute-start.6 = (bf16[512,2048]{1,0:T(8,128)(2,1)}, bf16[512,2048]{1,0:T(8,128)(2,1)}, u32[]{:S(2)}, u32[]{:S(2)}) collective-permute-start(bf16[512,2048]{1,0:T(8,128)(2,1)} %collective-permute-done.5), channel_id=1, source_target_pairs={{0,2},{1,3},{2,0},{3,1},{4,6},{5,7},{6,4},{7,5},{8,10},{9,11},{10,... | collective-permute-start | bytes 6291464 | tf_op jit(solution)/shard_map/ppermute | solution.py:464
  293.4 18.5 %copy-start.27 = (bf16[3,1024,512]{2,1,0:T(8,128)(2,1)S(1)}, bf16[3,1024,512]{2,1,0:T(8,128)(2,1)}, u32[]{:S(2)}) copy-start(bf16[3,1024,512]{2,1,0:T(8,128)(2,1)} %param.17) | copy-start | bytes 9437188
  344.9 16.5 %copy-start.11 = (bf16[3,1024,512]{2,1,0:T(8,128)(2,1)S(1)}, bf16[3,1024,512]{2,1,0:T(8,128)(2,1)}, u32[]{:S(2)}) copy-start(bf16[3,1024,512]{2,1,0:T(8,128)(2,1)} %attend_backward.3.by_oth.bx_oth) | copy-start | bytes 9437188
  357.7 1.3 collective-permute-start.19
  358.2 2.5 collective-permute-start.34
  358.4 14.1 %collective-permute-start.24 = (bf16[2,2,2,2,64,256]{5,4,3,2,1,0:T(8,128)(2,1)}, bf16[2,2,2,2,64,256]{5,4,3,2,1,0:T(8,128)(2,1)S(1)}, u32[]{:S(2)}, u32[]{:S(2)}) collective-permute-start(bf16[2,2,2,2,64,256]{5,4,3,2,1,0:T(8,128)(2,1)} %get-tuple-element.44), channel_id=1, source_target_pairs={{0,2},{1,3},{2,0},{3,1},{4,6},{5,7},{6,4},{7,5},{8,10},{9,11},{10,... | collective-permute-start | bytes 1572872 | tf_op jit(solution)/shard_map/ppermute | solution.py:464
  359.0 5.7 collective-permute-start.20
  360.8 5.5 collective-permute-start.35
  364.7 9.6 %collective-permute-start.29 = (bf16[2,2,2,2,64,256]{5,4,3,2,1,0:T(8,128)(2,1)S(1)}, bf16[2,2,2,2,64,256]{5,4,3,2,1,0:T(8,128)(2,1)S(1)}, u32[]{:S(2)}, u32[]{:S(2)}) collective-permute-start(bf16[2,2,2,2,64,256]{5,4,3,2,1,0:T(8,128)(2,1)S(1)} %copy-done.41), channel_id=1, source_target_pairs={{0,2},{1,3},{2,0},{3,1},{4,6},{5,7},{6,4},{7,5},{8,10},{9,11},{10,... | collective-permute-start | bytes 1572872 | tf_op jit(solution)/shard_map/ppermute | solution.py:464
  364.7 5.6 collective-permute-start.21
  366.3 5.7 collective-permute-start.36
  370.3 64.6 %collective-permute-start.49 = (bf16[2,2,2,2,64,1024]{5,4,3,2,1,0:T(8,128)(2,1)}, bf16[2,2,2,2,64,1024]{5,4,3,2,1,0:T(8,128)(2,1)}, u32[]{:S(2)}, u32[]{:S(2)}) collective-permute-start(bf16[2,2,2,2,64,1024]{5,4,3,2,1,0:T(8,128)(2,1)} %get-tuple-element.52), channel_id=1, source_target_pairs={{0,2},{1,3},{2,0},{3,1},{4,6},{5,7},{6,4},{7,5},{8,10},{9,11},{10,... | collective-permute-start | bytes 6291464 | tf_op jit(solution)/shard_map/ppermute | solution.py:464
  370.3 14.7 %collective-permute-start.22 = (f32[2048]{0:T(1024)S(1)}, f32[2048]{0:T(1024)S(1)}, u32[]{:S(2)}, u32[]{:S(2)}) collective-permute-start(f32[2048]{0:T(1024)S(1)} %add.532), channel_id=1, source_target_pairs={{0,8},{1,9},{2,10},{3,11},{4,12},{5,13},{6,14},{7,15},{8,0},{9,1},... | collective-permute-start | bytes 24584 | tf_op jit(solution)/shard_map/ppermute | solution.py:464
  372.0 13.0 %collective-permute-start.37 = (f32[10240]{0:T(1024)S(1)}, f32[10240]{0:T(1024)S(1)}, u32[]{:S(2)}, u32[]{:S(2)}) collective-permute-start(f32[10240]{0:T(1024)S(1)} %add.555), channel_id=1, source_target_pairs={{0,8},{1,9},{2,10},{3,11},{4,12},{5,13},{6,14},{7,15},{8,0},{9,1},... | collective-permute-start | bytes 122888 | tf_op jit(solution)/shard_map/ppermute | solution.py:464
  372.7 15.0 %collective-permute-start.25 = (bf16[2,2,2,64,256]{4,3,2,1,0:T(8,128)(2,1)S(1)}, bf16[2,2,2,64,256]{4,3,2,1,0:T(8,128)(2,1)S(1)}, u32[]{:S(2)}, u32[]{:S(2)}) collective-permute-start(bf16[2,2,2,64,256]{4,3,2,1,0:T(8,128)(2,1)S(1)} %get-tuple-element.121), channel_id=1, source_target_pairs={{0,1},{1,0},{2,3},{3,2},{4,5},{5,4},{6,7},{7,6},{8,9},{9,8},{10,11... | collective-permute-start | bytes 786440 | tf_op jit(solution)/shard_map/ppermute | solution.py:464
  374.5 13.7 %collective-permute-start.30 = (bf16[2,2,2,64,256]{4,3,2,1,0:T(8,128)(2,1)S(1)}, bf16[2,2,2,64,256]{4,3,2,1,0:T(8,128)(2,1)S(1)}, u32[]{:S(2)}, u32[]{:S(2)}) collective-permute-start(bf16[2,2,2,64,256]{4,3,2,1,0:T(8,128)(2,1)S(1)} %get-tuple-element.123), channel_id=1, source_target_pairs={{0,4},{1,5},{2,6},{3,7},{4,0},{5,1},{6,2},{7,3},{8,12},{9,13},{10,... | collective-permute-start | bytes 786440 | tf_op jit(solution)/shard_map/ppermute | solution.py:464
  385.0 54.1 %collective-permute-start.54 = (bf16[2,2,2,2,64,1024]{5,4,3,2,1,0:T(8,128)(2,1)}, bf16[2,2,2,2,64,1024]{5,4,3,2,1,0:T(8,128)(2,1)S(1)}, u32[]{:S(2)}, u32[]{:S(2)}) collective-permute-start(bf16[2,2,2,2,64,1024]{5,4,3,2,1,0:T(8,128)(2,1)} %get-tuple-element.54), channel_id=1, source_target_pairs={{0,2},{1,3},{2,0},{3,1},{4,6},{5,7},{6,4},{7,5},{8,10},{9,11},{10,... | collective-permute-start | bytes 6291464 | tf_op jit(solution)/shard_map/ppermute | solution.py:464
  385.0 25.3 %collective-permute-start.23 = (f32[2048]{0:T(1024)S(1)}, f32[2048]{0:T(1024)S(1)}, u32[]{:S(2)}, u32[]{:S(2)}) collective-permute-start(f32[2048]{0:T(1024)S(1)} %add.533), channel_id=1, source_target_pairs={{0,16},{1,17},{2,18},{3,19},{4,20},{5,21},{6,22},{7,23},{8,24},{9,... | collective-permute-start | bytes 24584 | tf_op jit(solution)/shard_map/ppermute | solution.py:464
  387.7 22.7 %collective-permute-start.38 = (f32[10240]{0:T(1024)S(1)}, f32[10240]{0:T(1024)S(1)}, u32[]{:S(2)}, u32[]{:S(2)}) collective-permute-start(f32[10240]{0:T(1024)S(1)} %add.556), channel_id=1, source_target_pairs={{0,16},{1,17},{2,18},{3,19},{4,20},{5,21},{6,22},{7,23},{8,24},{9,... | collective-permute-start | bytes 122888 | tf_op jit(solution)/shard_map/ppermute | solution.py:464
  388.2 5.4 collective-permute-start.26
  393.6 5.0 collective-permute-start.31
  398.5 5.0 collective-permute-start.27
  403.5 4.6 collective-permute-start.32
  408.1 4.8 collective-permute-start.28
  410.4 21.8 %collective-permute-start.9 = (bf16[2,2,2,2,64,768]{5,4,3,2,1,0:T(8,128)(2,1)}, bf16[2,2,2,2,64,768]{5,4,3,2,1,0:T(8,128)(2,1)S(1)}, u32[]{:S(2)}, u32[]{:S(2)}) collective-permute-start(bf16[2,2,2,2,64,768]{5,4,3,2,1,0:T(8,128)(2,1)} %get-tuple-element.40), channel_id=1, source_target_pairs={{0,2},{1,3},{2,0},{3,1},{4,6},{5,7},{6,4},{7,5},{8,10},{9,11},{10,... | collective-permute-start | bytes 4718600 | tf_op jit(solution)/shard_map/ppermute | solution.py:464
  410.4 22.9 %copy-start.21 = (bf16[2,2,2,2,64,768]{5,4,3,2,1,0:T(8,128)(2,1)S(1)}, bf16[2,2,2,2,64,768]{5,4,3,2,1,0:T(8,128)(2,1)}, u32[]{:S(2)}) copy-start(bf16[2,2,2,2,64,768]{5,4,3,2,1,0:T(8,128)(2,1)} %get-tuple-element.39) | copy-start | bytes 4718596
  410.5 23.4 %collective-permute-start.14 = (bf16[2,2,2,2,64,768]{5,4,3,2,1,0:T(8,128)(2,1)}, bf16[2,2,2,2,64,768]{5,4,3,2,1,0:T(8,128)(2,1)S(1)}, u32[]{:S(2)}, u32[]{:S(2)}) collective-permute-start(bf16[2,2,2,2,64,768]{5,4,3,2,1,0:T(8,128)(2,1)} %get-tuple-element.42), channel_id=1, source_target_pairs={{0,2},{1,3},{2,0},{3,1},{4,6},{5,7},{6,4},{7,5},{8,10},{9,11},{10,... | collective-permute-start | bytes 4718600 | tf_op jit(solution)/shard_map/ppermute | solution.py:464
  412.9 17.3 %collective-permute-start.33 = (bf16[64,256]{1,0:T(8,128)(2,1)S(1)}, bf16[64,256]{1,0:T(8,128)(2,1)S(1)}, u32[]{:S(2)}, u32[]{:S(2)}) collective-permute-start(bf16[64,256]{1,0:T(8,128)(2,1)S(1)} %fusion.128), channel_id=1, source_target_pairs={{0,16},{1,17},{2,18},{3,19},{4,20},{5,21},{6,22},{7,23},{8,24},{9,... | collective-permute-start | bytes 98312 | tf_op jit(solution)/shard_map/ppermute | solution.py:464
  430.2 12.7 %collective-permute-start.39 = (bf16[2,2,2,2,64,1024]{5,4,3,2,1,0:T(8,128)(2,1)}, bf16[2,2,2,2,64,1024]{5,4,3,2,1,0:T(8,128)(2,1)S(1)}, u32[]{:S(2)}, u32[]{:S(2)}) collective-permute-start(bf16[2,2,2,2,64,1024]{5,4,3,2,1,0:T(8,128)(2,1)} %get-tuple-element.48), channel_id=1, source_target_pairs={{0,2},{1,3},{2,0},{3,1},{4,6},{5,7},{6,4},{7,5},{8,10},{9,11},{10,... | collective-permute-start | bytes 6291464 | tf_op jit(solution)/shard_map/ppermute | solution.py:464
  432.1 24.0 %collective-permute-start.44 = (bf16[2,2,2,2,64,1024]{5,4,3,2,1,0:T(8,128)(2,1)}, bf16[2,2,2,2,64,1024]{5,4,3,2,1,0:T(8,128)(2,1)S(1)}, u32[]{:S(2)}, u32[]{:S(2)}) collective-permute-start(bf16[2,2,2,2,64,1024]{5,4,3,2,1,0:T(8,128)(2,1)} %get-tuple-element.50), channel_id=1, source_target_pairs={{0,2},{1,3},{2,0},{3,1},{4,6},{5,7},{6,4},{7,5},{8,10},{9,11},{10,... | collective-permute-start | bytes 6291464 | tf_op jit(solution)/shard_map/ppermute | solution.py:464
  433.8 20.5 %collective-permute-start.10 = (bf16[2,2,2,64,768]{4,3,2,1,0:T(8,128)(2,1)S(1)}, bf16[2,2,2,64,768]{4,3,2,1,0:T(8,128)(2,1)S(1)}, u32[]{:S(2)}, u32[]{:S(2)}) collective-permute-start(bf16[2,2,2,64,768]{4,3,2,1,0:T(8,128)(2,1)S(1)} %get-tuple-element.97), channel_id=1, source_target_pairs={{0,1},{1,0},{2,3},{3,2},{4,5},{5,4},{6,7},{7,6},{8,9},{9,8},{10,11... | collective-permute-start | bytes 2359304 | tf_op jit(solution)/shard_map/ppermute | solution.py:464
  434.9 20.5 %collective-permute-start.15 = (bf16[2,2,2,64,768]{4,3,2,1,0:T(8,128)(2,1)S(1)}, bf16[2,2,2,64,768]{4,3,2,1,0:T(8,128)(2,1)S(1)}, u32[]{:S(2)}, u32[]{:S(2)}) collective-permute-start(bf16[2,2,2,64,768]{4,3,2,1,0:T(8,128)(2,1)S(1)} %get-tuple-element.99), channel_id=1, source_target_pairs={{0,4},{1,5},{2,6},{3,7},{4,0},{5,1},{6,2},{7,3},{8,12},{9,13},{10,... | collective-permute-start | bytes 2359304 | tf_op jit(solution)/shard_map/ppermute | solution.py:464
  439.1 97.1 %collective-permute-start.50 = (bf16[2,2,2,64,1024]{4,3,2,1,0:T(8,128)(2,1)}, bf16[2,2,2,64,1024]{4,3,2,1,0:T(8,128)(2,1)}, u32[]{:S(2)}, u32[]{:S(2)}) collective-permute-start(bf16[2,2,2,64,1024]{4,3,2,1,0:T(8,128)(2,1)} %get-tuple-element.89), channel_id=1, source_target_pairs={{0,1},{1,0},{2,3},{3,2},{4,5},{5,4},{6,7},{7,6},{8,9},{9,8},{10,11... | collective-permute-start | bytes 3145736 | tf_op jit(solution)/shard_map/ppermute | solution.py:464
  442.9 95.7 %collective-permute-start.55 = (bf16[2,2,2,64,1024]{4,3,2,1,0:T(8,128)(2,1)}, bf16[2,2,2,64,1024]{4,3,2,1,0:T(8,128)(2,1)}, u32[]{:S(2)}, u32[]{:S(2)}) collective-permute-start(bf16[2,2,2,64,1024]{4,3,2,1,0:T(8,128)(2,1)} %get-tuple-element.91), channel_id=1, source_target_pairs={{0,4},{1,5},{2,6},{3,7},{4,0},{5,1},{6,2},{7,3},{8,12},{9,13},{10,... | collective-permute-start | bytes 3145736 | tf_op jit(solution)/shard_map/ppermute | solution.py:464
  454.3 86.4 %collective-permute-start.40 = (bf16[2,2,2,64,1024]{4,3,2,1,0:T(8,128)(2,1)}, bf16[2,2,2,64,1024]{4,3,2,1,0:T(8,128)(2,1)}, u32[]{:S(2)}, u32[]{:S(2)}) collective-permute-start(bf16[2,2,2,64,1024]{4,3,2,1,0:T(8,128)(2,1)} %get-tuple-element.93), channel_id=1, source_target_pairs={{0,1},{1,0},{2,3},{3,2},{4,5},{5,4},{6,7},{7,6},{8,9},{9,8},{10,11... | collective-permute-start | bytes 3145736 | tf_op jit(solution)/shard_map/ppermute | solution.py:464
  455.4 29.6 %collective-permute-start.11 = (bf16[2,2,64,768]{3,2,1,0:T(8,128)(2,1)S(1)}, bf16[2,2,64,768]{3,2,1,0:T(8,128)(2,1)S(1)}, u32[]{:S(2)}, u32[]{:S(2)}) collective-permute-start(bf16[2,2,64,768]{3,2,1,0:T(8,128)(2,1)S(1)} %get-tuple-element.109), channel_id=1, source_target_pairs={{0,4},{1,5},{2,6},{3,7},{4,0},{5,1},{6,2},{7,3},{8,12},{9,13},{10,... | collective-permute-start | bytes 1179656 | tf_op jit(solution)/shard_map/ppermute | solution.py:464
  456.2 50.5 %collective-permute-start.16 = (bf16[2,2,64,768]{3,2,1,0:T(8,128)(2,1)S(1)}, bf16[2,2,64,768]{3,2,1,0:T(8,128)(2,1)S(1)}, u32[]{:S(2)}, u32[]{:S(2)}) collective-permute-start(bf16[2,2,64,768]{3,2,1,0:T(8,128)(2,1)S(1)} %get-tuple-element.111), channel_id=1, source_target_pairs={{0,1},{1,0},{2,3},{3,2},{4,5},{5,4},{6,7},{7,6},{8,9},{9,8},{10,11... | collective-permute-start | bytes 1179656 | tf_op jit(solution)/shard_map/ppermute | solution.py:464
  485.0 58.8 %collective-permute-start.45 = (bf16[2,2,2,64,1024]{4,3,2,1,0:T(8,128)(2,1)}, bf16[2,2,2,64,1024]{4,3,2,1,0:T(8,128)(2,1)}, u32[]{:S(2)}, u32[]{:S(2)}) collective-permute-start(bf16[2,2,2,64,1024]{4,3,2,1,0:T(8,128)(2,1)} %get-tuple-element.95), channel_id=1, source_target_pairs={{0,4},{1,5},{2,6},{3,7},{4,0},{5,1},{6,2},{7,3},{8,12},{9,13},{10,... | collective-permute-start | bytes 3145736 | tf_op jit(solution)/shard_map/ppermute | solution.py:464
  506.7 6.9 %collective-permute-start.12 = (bf16[2,64,768]{2,1,0:T(8,128)(2,1)S(1)}, bf16[2,64,768]{2,1,0:T(8,128)(2,1)S(1)}, u32[]{:S(2)}, u32[]{:S(2)}) collective-permute-start(bf16[2,64,768]{2,1,0:T(8,128)(2,1)S(1)} %get-tuple-element.125), channel_id=1, source_target_pairs={{0,8},{1,9},{2,10},{3,11},{4,12},{5,13},{6,14},{7,15},{8,0},{9,1},... | collective-permute-start | bytes 589832 | tf_op jit(solution)/shard_map/ppermute | solution.py:464
  513.6 6.0 %collective-permute-start.17 = (bf16[2,64,768]{2,1,0:T(8,128)(2,1)S(1)}, bf16[2,64,768]{2,1,0:T(8,128)(2,1)S(1)}, u32[]{:S(2)}, u32[]{:S(2)}) collective-permute-start(bf16[2,64,768]{2,1,0:T(8,128)(2,1)S(1)} %get-tuple-element.127), channel_id=1, source_target_pairs={{0,8},{1,9},{2,10},{3,11},{4,12},{5,13},{6,14},{7,15},{8,0},{9,1},... | collective-permute-start | bytes 589832 | tf_op jit(solution)/shard_map/ppermute | solution.py:464
  519.6 5.5 collective-permute-start.13
  525.1 5.6 collective-permute-start.18
  537.9 14.9 %collective-permute-start.51 = (bf16[2,2,64,1024]{3,2,1,0:T(8,128)(2,1)S(1)}, bf16[2,2,64,1024]{3,2,1,0:T(8,128)(2,1)S(1)}, u32[]{:S(2)}, u32[]{:S(2)}) collective-permute-start(bf16[2,2,64,1024]{3,2,1,0:T(8,128)(2,1)S(1)} %get-tuple-element.101), channel_id=1, source_target_pairs={{0,4},{1,5},{2,6},{3,7},{4,0},{5,1},{6,2},{7,3},{8,12},{9,13},{10,... | collective-permute-start | bytes 1572872 | tf_op jit(solution)/shard_map/ppermute | solution.py:464
  540.1 14.9 %collective-permute-start.56 = (bf16[2,2,64,1024]{3,2,1,0:T(8,128)(2,1)S(1)}, bf16[2,2,64,1024]{3,2,1,0:T(8,128)(2,1)S(1)}, u32[]{:S(2)}, u32[]{:S(2)}) collective-permute-start(bf16[2,2,64,1024]{3,2,1,0:T(8,128)(2,1)S(1)} %get-tuple-element.103), channel_id=1, source_target_pairs={{0,1},{1,0},{2,3},{3,2},{4,5},{5,4},{6,7},{7,6},{8,9},{9,8},{10,11... | collective-permute-start | bytes 1572872 | tf_op jit(solution)/shard_map/ppermute | solution.py:464
  542.3 18.7 %collective-permute-start.41 = (bf16[2,2,64,1024]{3,2,1,0:T(8,128)(2,1)S(1)}, bf16[2,2,64,1024]{3,2,1,0:T(8,128)(2,1)S(1)}, u32[]{:S(2)}, u32[]{:S(2)}) collective-permute-start(bf16[2,2,64,1024]{3,2,1,0:T(8,128)(2,1)S(1)} %get-tuple-element.105), channel_id=1, source_target_pairs={{0,4},{1,5},{2,6},{3,7},{4,0},{5,1},{6,2},{7,3},{8,12},{9,13},{10,... | collective-permute-start | bytes 1572872 | tf_op jit(solution)/shard_map/ppermute | solution.py:464
  545.5 17.5 %collective-permute-start.46 = (bf16[2,2,64,1024]{3,2,1,0:T(8,128)(2,1)S(1)}, bf16[2,2,64,1024]{3,2,1,0:T(8,128)(2,1)S(1)}, u32[]{:S(2)}, u32[]{:S(2)}) collective-permute-start(bf16[2,2,64,1024]{3,2,1,0:T(8,128)(2,1)S(1)} %get-tuple-element.107), channel_id=1, source_target_pairs={{0,1},{1,0},{2,3},{3,2},{4,5},{5,4},{6,7},{7,6},{8,9},{9,8},{10,11... | collective-permute-start | bytes 1572872 | tf_op jit(solution)/shard_map/ppermute | solution.py:464
  553.0 10.5 %collective-permute-start.52 = (bf16[2,64,1024]{2,1,0:T(8,128)(2,1)S(1)}, bf16[2,64,1024]{2,1,0:T(8,128)(2,1)S(1)}, u32[]{:S(2)}, u32[]{:S(2)}) collective-permute-start(bf16[2,64,1024]{2,1,0:T(8,128)(2,1)S(1)} %get-tuple-element.113), channel_id=1, source_target_pairs={{0,8},{1,9},{2,10},{3,11},{4,12},{5,13},{6,14},{7,15},{8,0},{9,1},... | collective-permute-start | bytes 786440 | tf_op jit(solution)/shard_map/ppermute | solution.py:464
  555.3 9.5 %collective-permute-start.57 = (bf16[2,64,1024]{2,1,0:T(8,128)(2,1)S(1)}, bf16[2,64,1024]{2,1,0:T(8,128)(2,1)S(1)}, u32[]{:S(2)}, u32[]{:S(2)}) collective-permute-start(bf16[2,64,1024]{2,1,0:T(8,128)(2,1)S(1)} %get-tuple-element.115), channel_id=1, source_target_pairs={{0,8},{1,9},{2,10},{3,11},{4,12},{5,13},{6,14},{7,15},{8,0},{9,1},... | collective-permute-start | bytes 786440 | tf_op jit(solution)/shard_map/ppermute | solution.py:464
  561.2 12.9 %collective-permute-start.42 = (bf16[2,64,1024]{2,1,0:T(8,128)(2,1)S(1)}, bf16[2,64,1024]{2,1,0:T(8,128)(2,1)S(1)}, u32[]{:S(2)}, u32[]{:S(2)}) collective-permute-start(bf16[2,64,1024]{2,1,0:T(8,128)(2,1)S(1)} %get-tuple-element.117), channel_id=1, source_target_pairs={{0,8},{1,9},{2,10},{3,11},{4,12},{5,13},{6,14},{7,15},{8,0},{9,1},... | collective-permute-start | bytes 786440 | tf_op jit(solution)/shard_map/ppermute | solution.py:464
  563.2 16.4 %collective-permute-start.47 = (bf16[2,64,1024]{2,1,0:T(8,128)(2,1)S(1)}, bf16[2,64,1024]{2,1,0:T(8,128)(2,1)S(1)}, u32[]{:S(2)}, u32[]{:S(2)}) collective-permute-start(bf16[2,64,1024]{2,1,0:T(8,128)(2,1)S(1)} %get-tuple-element.119), channel_id=1, source_target_pairs={{0,8},{1,9},{2,10},{3,11},{4,12},{5,13},{6,14},{7,15},{8,0},{9,1},... | collective-permute-start | bytes 786440 | tf_op jit(solution)/shard_map/ppermute | solution.py:464
  563.6 16.8 %collective-permute-start.53 = (bf16[64,1024]{1,0:T(8,128)(2,1)S(1)}, bf16[64,1024]{1,0:T(8,128)(2,1)S(1)}, u32[]{:S(2)}, u32[]{:S(2)}) collective-permute-start(bf16[64,1024]{1,0:T(8,128)(2,1)S(1)} %fusion.108), channel_id=1, source_target_pairs={{0,16},{1,17},{2,18},{3,19},{4,20},{5,21},{6,22},{7,23},{8,24},{9,... | collective-permute-start | bytes 393224 | tf_op jit(solution)/shard_map/ppermute | solution.py:464
  564.9 22.6 %collective-permute-start.58 = (bf16[64,1024]{1,0:T(8,128)(2,1)S(1)}, bf16[64,1024]{1,0:T(8,128)(2,1)S(1)}, u32[]{:S(2)}, u32[]{:S(2)}) collective-permute-start(bf16[64,1024]{1,0:T(8,128)(2,1)S(1)} %fusion.110), channel_id=1, source_target_pairs={{0,16},{1,17},{2,18},{3,19},{4,20},{5,21},{6,22},{7,23},{8,24},{9,... | collective-permute-start | bytes 393224 | tf_op jit(solution)/shard_map/ppermute | solution.py:464
  574.1 15.4 %collective-permute-start.43 = (bf16[64,1024]{1,0:T(8,128)(2,1)S(1)}, bf16[64,1024]{1,0:T(8,128)(2,1)S(1)}, u32[]{:S(2)}, u32[]{:S(2)}) collective-permute-start(bf16[64,1024]{1,0:T(8,128)(2,1)S(1)} %fusion.104), channel_id=1, source_target_pairs={{0,16},{1,17},{2,18},{3,19},{4,20},{5,21},{6,22},{7,23},{8,24},{9,... | collective-permute-start | bytes 393224 | tf_op jit(solution)/shard_map/ppermute | solution.py:464
  579.6 11.4 %collective-permute-start.48 = (bf16[64,1024]{1,0:T(8,128)(2,1)S(1)}, bf16[64,1024]{1,0:T(8,128)(2,1)S(1)}, u32[]{:S(2)}, u32[]{:S(2)}) collective-permute-start(bf16[64,1024]{1,0:T(8,128)(2,1)S(1)} %fusion.106), channel_id=1, source_target_pairs={{0,16},{1,17},{2,18},{3,19},{4,20},{5,21},{6,22},{7,23},{8,24},{9,... | collective-permute-start | bytes 393224 | tf_op jit(solution)/shard_map/ppermute | solution.py:464
  (40 other events, 296.0 us)

commit v2 on v0

--- a/solution.py
+++ b/solution.py
@@ -1,6 +1,10 @@
+import functools
+
 import jax
 import jax.numpy as jnp
 from jax import lax
+from jax.experimental import pallas as pl
+from jax.experimental.pallas import tpu as pltpu
 from jax.sharding import PartitionSpec as P
 
 D = 1024
@@ -66,7 +70,7 @@
     return (grad_q.astype(jnp.bfloat16), grad_k.astype(jnp.bfloat16), grad_v.astype(jnp.bfloat16))
 
 
-def body(
+def body_tensor(
     tokens,
     cotangent,
     w_qkv,
@@ -216,6 +220,777 @@
     )
 
 
+AXES = ("dp", "tensor")
+LOG2E = 1.4426950408889634
+VMEM = 56 * 1024 * 1024
+NT = (((1,), (1,)), ((), ()))
+
+
+def dot(left, right):
+    return jnp.dot(left, right, preferred_element_type=jnp.float32)
+
+
+def dot_nt(left, right):
+    return lax.dot_general(left, right, NT, preferred_element_type=jnp.float32)
+
+
+def head_masks(width):
+    lane = lax.broadcasted_iota(jnp.int32, (1, width), 1)
+    return lane < HEAD_DIM
+
+
+def attend_kernel(q_ref, k_ref, v_ref, c_ref, l_ref):
+    width = q_ref.shape[1]
+    first = head_masks(128)
+    for pair in range(width // 128):
+        cols = slice(pair * 128, pair * 128 + 128)
+        queries, key_rows = q_ref[:, cols], k_ref[:, cols]
+        values_t = v_ref[:, cols].T
+        parts = []
+        for head in range(2):
+            mask = first if head == 0 else jnp.logical_not(first)
+            picked = jnp.where(mask, queries, jnp.zeros_like(queries))
+            scores = dot_nt(key_rows, picked) * (LOG2E * HEAD_DIM**-0.5)
+            peak = jnp.max(scores, axis=0, keepdims=True)
+            lifted = jnp.exp2(scores - peak)
+            totals = jnp.sum(lifted, axis=0, keepdims=True)
+            context = dot(
+                values_t[head * HEAD_DIM : (head + 1) * HEAD_DIM], lifted.astype(jnp.bfloat16)
+            )
+            parts.append(context * (1.0 / totals))
+            l_ref[0, pair * 2 + head : pair * 2 + head + 1, :] = peak + jnp.log2(totals)
+        c_ref[:, cols] = jnp.concatenate(parts, axis=0).T.astype(jnp.bfloat16)
+
+
+def attend_forward(queries, key_rows, values):
+    rows, width = queries.shape
+    block = min(width, 512)
+    heads = block // HEAD_DIM
+    seqs, groups = rows // SEQ, width // block
+    spec = pl.BlockSpec((SEQ, block), lambda s, g: (s, g))
+    return pl.pallas_call(
+        attend_kernel,
+        grid=(seqs, groups),
+        in_specs=[spec] * 3,
+        out_specs=[spec, pl.BlockSpec((1, heads, SEQ), lambda s, g: (s * groups + g, 0, 0))],
+        out_shape=[
+            jax.ShapeDtypeStruct((rows, width), jnp.bfloat16),
+            jax.ShapeDtypeStruct((seqs * groups, heads, SEQ), jnp.float32),
+        ],
+        compiler_params=pltpu.CompilerParams(vmem_limit_bytes=VMEM),
+        cost_estimate=pl.CostEstimate(
+            flops=rows * width * SEQ * 4, bytes_accessed=rows * width * 8, transcendentals=rows * SEQ * width // HEAD_DIM
+        ),
+        name="attend_forward",
+    )(queries, key_rows, values)
+
+
+MESH = pl.DeviceIdType.MESH
+CHUNKS = 8
+SPAN = 256
+
+
+def bit_of(index, bit):
+    return lax.rem(lax.div(index, bit), 2)
+
+
+def flip(index, bit):
+    return index + bit - 2 * bit * bit_of(index, bit)
+
+
+def mine():
+    return lax.axis_index("dp"), lax.axis_index("tensor")
+
+
+def greet():
+    dp, t = mine()
+    barrier = pltpu.get_barrier_semaphore()
+    peers = [(flip(dp, 1), t), (dp, flip(t, 1)), (flip(dp, 2), t), (flip(dp, 4), t), (flip(dp, 8), t)]
+    for peer in peers:
+        pl.semaphore_signal(barrier, inc=1, device_id=peer, device_id_type=MESH)
+    pl.semaphore_wait(barrier, len(peers))
+
+
+def turn(left_ref, turned):
+    dp, _ = mine()
+    height = turned.shape[0] // 16
+    whole = left_ref[...].T
+    for piece in range(16):
+        spot = 0
+        for bit, weight in ((1, 8), (2, 4), (4, 2), (8, 1)):
+            own = bit_of(dp, bit)
+            spot = spot + weight * (own if piece & bit else 1 - own)
+        turned[pl.ds(pl.multiple_of(spot * height, height), height), :] = whole[
+            piece * height : (piece + 1) * height
+        ]
+
+
+class Scatter:
+    def __init__(self, keep, lands, sems):
+        self.keep = keep
+        self.lands = lands
+        self.sent, self.got = sems
+
+    def copy(self, stage, m):
+        dp, t = mine()
+        odd = lax.rem(m, 2)
+        rows = self.keep.shape[3]
+        if stage == 1:
+            src, peer = self.keep.at[m, 0], (dp + odd * (flip(dp, 2) - dp), t + (1 - odd) * (1 - 2 * t))
+        elif stage == 2:
+            src, peer = self.keep.at[m, 1, 0], (dp + (1 - odd) * (flip(dp, 2) - dp), t + odd * (1 - 2 * t))
+        elif stage == 3:
+            src, peer = self.keep.at[m, 1, 1, pl.ds(0, rows // 2)], (flip(dp, 4), t)
+        else:
+            src, peer = self.keep.at[m, 1, 1, pl.ds(rows // 2, rows // 4)], (flip(dp, 8), t)
+        return pltpu.make_async_remote_copy(
+            src_ref=src,
+            dst_ref=self.lands[stage - 1].at[m],
+            send_sem=self.sent.at[stage, m],
+            recv_sem=self.got.at[stage, m],
+            device_id=peer,
+            device_id_type=MESH,
+        )
+
+    def add(self, stage, m):
+        rows = self.keep.shape[3]
+        self.copy(stage, m).wait_recv()
+        land = self.lands[stage - 1]
+        if stage == 1:
+            self.keep[m, 1] = plus(self.keep[m, 1], land[m])
+        elif stage == 2:
+            self.keep[m, 1, 1] = plus(self.keep[m, 1, 1], land[m])
+        elif stage == 3:
+            half = pl.ds(rows // 2, rows // 2)
+            self.keep[m, 1, 1, half] = plus(self.keep[m, 1, 1, half], land[m])
+
+    def last(self, m):
+        rows = self.keep.shape[3]
+        self.copy(4, m).wait_recv()
+        rest = pl.ds(3 * rows // 4, rows // 4)
+        return self.keep[m, 1, 1, rest].astype(jnp.float32) + self.lands[3][m].astype(jnp.float32)
+
+    def drain(self, m):
+        for stage in (1, 2, 3, 4):
+            self.copy(stage, m).wait_send()
+
+
+class Pair:
+    def __init__(self, keep, send, land, sems):
+        self.keep, self.send, self.land = keep, send, land
+        self.sent, self.got = sems
+
+    def copy(self, m):
+        dp, t = mine()
+        return pltpu.make_async_remote_copy(
+            src_ref=self.send.at[lax.rem(m, 2)],
+            dst_ref=self.land.at[m],
+            send_sem=self.sent.at[0, m],
+            recv_sem=self.got.at[0, m],
+            device_id=(flip(dp, 1), t),
+            device_id_type=MESH,
+        )
+
+    def store(self, m, product, own):
+        half = product.shape[0] // 2
+        rows = half // 2
+        odd = lax.rem(m, 2)
+        for x in range(2):
+            first = odd * x + (1 - odd) * own
+            second = odd * own + (1 - odd) * x
+            self.send[odd, first, second] = product[x * rows : (x + 1) * rows].astype(jnp.bfloat16)
+            self.keep[m, first, second] = product[half + x * rows : half + (x + 1) * rows].astype(
+                jnp.bfloat16
+            )
+
+    def free(self, m):
+        @pl.when(m >= 2)
+        def _():
+            self.copy(m - 2).wait_send()
+
+    def add(self, m):
+        self.copy(m).wait_recv()
+        for a in range(2):
+            for b in range(2):
+                self.keep[m, a, b] = plus(self.keep[m, a, b], self.land[m, a, b])
+
+
+def plus(left, right):
+    return (left.astype(jnp.float32) + right.astype(jnp.float32)).astype(jnp.bfloat16)
+
+
+def scatter_scratch(chunks, rows, width, pair):
+    def buffer(*shape):
+        return pltpu.VMEM(shape, jnp.bfloat16)
+
+    out = [buffer(chunks, 2, 2, rows, width)]
+    if pair:
+        out += [buffer(2, 2, 2, rows, width), buffer(chunks, 2, 2, rows, width)]
+    return out
+
+
+def land_scratch(chunks, rows, width):
+    def buffer(*shape):
+        return pltpu.VMEM(shape, jnp.bfloat16)
+
+    return [
+        buffer(chunks, 2, rows, width),
+        buffer(chunks, rows, width),
+        buffer(chunks, rows // 2, width),
+        buffer(chunks, rows // 4, width),
+    ]
+
+
+def guarded(low, high, m, action):
+    @pl.when(jnp.logical_and(m >= low, m < high))
+    def _():
+        action(m)
+
+
+def ffn_back_kernel(
+    dm_ref, hr_ref, g_own, g_oth, s_own, s_oth, wd_own, wd_oth, wu_own, wu_oth,
+    down_ref, bias_ref, up_hbm, dh_hbm,
+    dm_turned, hr_turned, total,
+    keep_d, send_d, land_d, d1, d2, d3, d4, keep_u, send_u, land_u,
+    sent_d, got_d, sent_u, got_u, local_u, local_h,
+):
+    j = pl.program_id(0)
+    chunks = pl.num_programs(0)
+    pair_d = Pair(keep_d, send_d, land_d, (sent_d, got_d))
+    pair_u = Pair(keep_u, send_u, land_u, (sent_u, got_u))
+    scatter = Scatter(keep_d, (d1, d2, d3, d4), (sent_d, got_d))
+
+    @pl.when(j == 0)
+    def _():
+        greet()
+        turn(dm_ref, dm_turned)
+        turn(hr_ref, hr_turned)
+        total[...] = jnp.zeros_like(total)
+
+    def out_copy(m):
+        return pltpu.make_async_copy(keep_u.at[m], up_hbm.at[m], local_u.at[m])
+
+    def finish(m):
+        width = keep_d.shape[4]
+        down_ref[pl.ds(pl.multiple_of(m * width, width), width), :] = scatter.last(m).T
+
+    def pair_down(m):
+        pair_d.add(m)
+        scatter.copy(1, m).start()
+
+    def pair_up(m):
+        pair_u.add(m)
+        out_copy(m).start()
+
+    def step(stage):
+        def run(m):
+            scatter.add(stage, m)
+            scatter.copy(stage + 1, m).start()
+
+        return run
+
+    def tick(n):
+        guarded(0, chunks, n - 1, pair_down)
+        guarded(0, chunks, n - 1, pair_up)
+        guarded(0, chunks, n - 3, step(1))
+        guarded(0, chunks, n - 5, step(2))
+        guarded(0, chunks, n - 6, step(3))
+        guarded(0, chunks, n - 7, finish)
+
+    pair_d.free(j)
+    for own, g_ref in ((0, g_oth), (1, g_own)):
+        pair_d.store(j, dot(dm_turned[...], g_ref[...]), own)
+    pair_d.copy(j).start()
+    low = []
+    for own, slope, weight in ((0, s_oth, wd_oth), (1, s_own, wd_own)):
+        raised = dot_nt(dm_ref[...], weight[...]) * slope[...].astype(jnp.float32)
+        low.append(raised.astype(jnp.bfloat16))
+        bias_ref[own, pl.ds(j, 1), :] = jnp.sum(low[-1].astype(jnp.float32), axis=0, keepdims=True)
+    pair_u.free(j)
+    for own in range(2):
+        pair_u.store(j, dot(hr_turned[...], low[own]), own)
+    pair_u.copy(j).start()
+    total[...] += dot_nt(low[0], wu_oth[...]) + dot_nt(low[1], wu_own[...])
+    tick(j)
+
+    @pl.when(j == chunks - 1)
+    def _():
+        out = pltpu.make_async_copy(total, dh_hbm, local_h)
+        out.start()
+
+        @pl.loop(0, 7)
+        def _(extra):
+            tick(chunks + extra)
+
+        for m in range(max(0, CHUNKS - 2), CHUNKS):
+            pair_d.copy(m).wait_send()
+            pair_u.copy(m).wait_send()
+
+        @pl.loop(0, CHUNKS)
+        def _(m):
+            scatter.drain(m)
+            out_copy(m).wait()
+
+        out.wait()
+
+
+def ffn_backward(grad_branch, hidden_rows, act, act2, slope, slope2, w_down, w_down2, w_up, w_up2):
+    rows, depth = grad_branch.shape
+    inner = act.shape[1]
+    tile = inner // CHUNKS
+    whole = pl.BlockSpec((rows, depth), lambda j: (0, 0))
+    column = pl.BlockSpec((rows, tile), lambda j: (0, j))
+    row = pl.BlockSpec((tile, depth), lambda j: (j, 0))
+    weight_column = pl.BlockSpec((depth, tile), lambda j: (0, j))
+    sems = pltpu.SemaphoreType.DMA((5, CHUNKS))
+    return pl.pallas_call(
+        ffn_back_kernel,
+        grid=(CHUNKS,),
+        in_specs=[whole, whole, column, column, column, column, row, row, weight_column, weight_column],
+        out_specs=[
+            pl.BlockSpec((inner, depth // 16), lambda j: (0, 0)),
+            pl.BlockSpec((2, CHUNKS, tile), lambda j: (0, 0, 0)),
+            pl.BlockSpec(memory_space=pl.ANY),
+            pl.BlockSpec(memory_space=pl.ANY),
+        ],
+        out_shape=[
+            jax.ShapeDtypeStruct((inner, depth // 16), jnp.float32),
+            jax.ShapeDtypeStruct((2, CHUNKS, tile), jnp.float32),
+            jax.ShapeDtypeStruct((CHUNKS, 2, 2, SPAN, tile), jnp.bfloat16),
+            jax.ShapeDtypeStruct((rows, depth), jnp.float32),
+        ],
+        scratch_shapes=[
+            pltpu.VMEM((depth, rows), jnp.bfloat16),
+            pltpu.VMEM((depth, rows), jnp.bfloat16),
+            pltpu.VMEM((rows, depth), jnp.float32),
+            *scatter_scratch(CHUNKS, SPAN, tile, True),
+            *land_scratch(CHUNKS, SPAN, tile),
+            *scatter_scratch(CHUNKS, SPAN, tile, True),
+            sems, sems, sems, sems,
+            pltpu.SemaphoreType.DMA((CHUNKS,)),
+            pltpu.SemaphoreType.DMA,
+        ],
+        compiler_params=pltpu.CompilerParams(
+            vmem_limit_bytes=VMEM, collective_id=1, has_side_effects=True
+        ),
+        cost_estimate=pl.CostEstimate(
+            flops=rows * depth * inner * 16, bytes_accessed=60 * 1024 * 1024, transcendentals=0
+        ),
+        name="ffn_backward",
+    )(grad_branch, hidden_rows, act, act2, slope, slope2, w_down, w_down2, w_up, w_up2)
+
+
+def attend_back_one(queries, key_rows, values, grad_ctx, levels):
+    scale = HEAD_DIM**-0.5
+    first = head_masks(128)
+    keys_t = key_rows.T
+    parts = []
+    grad_k = grad_v = None
+    for head in range(2):
+        mask = first if head == 0 else jnp.logical_not(first)
+        picked = jnp.where(mask, queries, jnp.zeros_like(queries))
+        grad_picked = jnp.where(mask, grad_ctx, jnp.zeros_like(grad_ctx))
+        weights = jnp.exp2(dot_nt(key_rows, picked) * (LOG2E * scale) - levels[head])
+        grad_weights = dot_nt(values, grad_picked)
+        rowsum = jnp.sum(weights * grad_weights, axis=0, keepdims=True)
+        grad_low = (weights * (grad_weights - rowsum)).astype(jnp.bfloat16)
+        piece_v = dot(weights.astype(jnp.bfloat16), grad_picked)
+        piece_k = dot(grad_low, picked)
+        grad_v = piece_v if grad_v is None else grad_v + piece_v
+        grad_k = piece_k if grad_k is None else grad_k + piece_k
+        parts.append(dot(keys_t[head * HEAD_DIM : (head + 1) * HEAD_DIM], grad_low))
+    grad_q = jnp.concatenate(parts, axis=0).T
+    return (
+        (grad_q * scale).astype(jnp.bfloat16),
+        (grad_k * scale).astype(jnp.bfloat16),
+        grad_v.astype(jnp.bfloat16),
+    )
+
+
+class Total:
+    def __init__(self, sums, lands, sems):
+        self.sums, self.lands = sums, lands
+        self.sent, self.got = sems
+
+    def copy(self, stage):
+        dp, t = mine()
+        peer = ((flip(dp, 1), t), (dp, 1 - t), (flip(dp, 2), t), (flip(dp, 4), t), (flip(dp, 8), t))[stage]
+        return pltpu.make_async_remote_copy(
+            src_ref=self.sums.at[stage],
+            dst_ref=self.lands.at[stage],
+            send_sem=self.sent.at[stage],
+            recv_sem=self.got.at[stage],
+            device_id=peer,
+            device_id_type=MESH,
+        )
+
+    def step(self, stage):
+        self.copy(stage).wait_recv()
+        self.sums[stage + 1] = self.sums[stage] + self.lands[stage]
+        if stage < 4:
+            self.copy(stage + 1).start()
+
+    def drain(self):
+        for stage in range(5):
+            self.copy(stage).wait_send()
+
+
+def attend_back_kernel(
+    da_ref, x_ref, up_hbm, dz_hbm, vec_ref, l_own, l_oth,
+    q_own, k_own, v_own, c_own, wo_own, wq_own,
+    q_oth, k_oth, v_oth, c_oth, wo_oth, wq_oth,
+    gin_hbm, gup_ref, gout_ref, gqkv_ref, vec_out, bias_out,
+    da_turned, x_turned, total, stack,
+    keep_u, u1, u2, u3, u4,
+    keep_a, send_a, land_a, a1, a2, a3, a4,
+    vec_sums, vec_lands, bias_sums, bias_lands,
+    sent_u, got_u, sent_a, got_a, sent_v, got_v, sent_b, got_b, local_u, local_z, local_g,
+):
+    g = pl.program_id(0)
+    steps = pl.num_programs(0)
+    seqs = x_ref.shape[0] // SEQ
+    pair = Pair(keep_a, send_a, land_a, (sent_a, got_a))
+    scatter_a = Scatter(keep_a, (a1, a2, a3, a4), (sent_a, got_a))
+    scatter_u = Scatter(keep_u, (u1, u2, u3, u4), (sent_u, got_u))
+    vec_total = Total(vec_sums, vec_lands, (sent_v, got_v))
+    bias_total = Total(bias_sums, bias_lands, (sent_b, got_b))
+
+    def load_up(m):
+        return pltpu.make_async_copy(up_hbm.at[m], keep_u.at[m], local_u.at[m])
+
+    load_z = pltpu.make_async_copy(dz_hbm, total, local_z)
+
+    @pl.when(g == 0)
+    def _():
+        for m in range(CHUNKS):
+            load_up(m).start()
+        load_z.start()
+        greet()
+        for m in range(CHUNKS):
+            load_up(m).wait()
+            scatter_u.copy(1, m).start()
+        vec_sums[0] = vec_ref[...]
+        vec_total.copy(0).start()
+        turn(x_ref, x_turned)
+        turn(da_ref, da_turned)
+        load_z.wait()
+
+    def finish_u(m):
+        width = keep_u.shape[4]
+        gup_ref[:, pl.ds(pl.multiple_of(m * width, width), width)] = scatter_u.last(m)
+
+    def finish_a(m):
+        done = scatter_a.last(m)
+        where = lax.div(m, 2)
+        width = done.shape[1] // 2
+        cols = pl.ds(pl.multiple_of(where * width, width), width)
+
+        @pl.when(lax.rem(m, 2) == 0)
+        def _():
+            gout_ref[cols, :] = done[:, :width].T
+            gqkv_ref[0, :, cols] = done[:, width:]
+
+        @pl.when(lax.rem(m, 2) == 1)
+        def _():
+            gqkv_ref[1, :, cols] = done[:, :width]
+            gqkv_ref[2, :, cols] = done[:, width:]
+
+    def pair_a(m):
+        pair.add(m)
+        scatter_a.copy(1, m).start()
+
+    def step(scatter, stage):
+        def run(m):
+            scatter.add(stage, m)
+            scatter.copy(stage + 1, m).start()
+
+        return run
+
+    def tick_u(n):
+        guarded(0, CHUNKS, n, step(scatter_u, 1))
+        guarded(0, CHUNKS, n - 1, step(scatter_u, 2))
+        guarded(0, CHUNKS, n - 2, step(scatter_u, 3))
+        guarded(0, CHUNKS, n - 3, finish_u)
+
+    def tick_a(n):
+        guarded(0, CHUNKS, n, pair_a)
+        guarded(0, CHUNKS, n - 2, step(scatter_a, 1))
+        guarded(0, CHUNKS, n - 3, step(scatter_a, 2))
+        guarded(0, CHUNKS, n - 4, step(scatter_a, 3))
+        guarded(0, CHUNKS, n - 5, finish_a)
+
+    _, t = mine()
+    sides = (
+        (0, q_oth, k_oth, v_oth, c_oth, l_oth, wo_oth),
+        (1, q_own, k_own, v_own, c_own, l_own, wo_own),
+    )
+    for own, q_ref, k_ref, v_ref, _, l_ref, wo_ref in sides:
+        grad_ctx = dot_nt(da_ref[...], wo_ref[...]).astype(jnp.bfloat16)
+        for s in range(seqs):
+            rows = slice(s * SEQ, (s + 1) * SEQ)
+            levels = [l_ref[s, pl.ds(2 * g + head, 1), :] for head in range(2)]
+            grads = attend_back_one(
+                q_ref[rows, :], k_ref[rows, :], v_ref[rows, :], grad_ctx[rows], levels
+            )
+            for kind in range(3):
+                stack[rows, (own * 3 + kind) * 128 : (own * 3 + kind + 1) * 128] = grads[kind]
+        spot = t * own + (1 - t) * (1 - own)
+        for kind, base in ((0, 0), (2, 8)):
+            piece = stack[:, (own * 3 + kind) * 128 : (own * 3 + kind + 1) * 128]
+            bias_sums[0, pl.ds(base + spot * 4 + g, 1), :] = jnp.sum(
+                piece.astype(jnp.float32), axis=0, keepdims=True
+            )
+        tick_u(3 * g + own)
+    pair.free(2 * g)
+    for own, _, _, _, c_ref, _, _ in sides:
+        first = dot(da_turned[...], c_ref[...])
+        second = dot(x_turned[...], stack[:, own * 384 : own * 384 + 128])
+        pair.store(2 * g, jnp.concatenate([first, second], axis=1), own)
+    pair.copy(2 * g).start()
+    pair.free(2 * g + 1)
+    for own in range(2):
+        pair.store(2 * g + 1, dot(x_turned[...], stack[:, own * 384 + 128 : own * 384 + 384]), own)
+    pair.copy(2 * g + 1).start()
+    weights = [wq_oth[kind] for kind in range(3)] + [wq_own[kind] for kind in range(3)]
+    total[...] += dot_nt(stack[...], jnp.concatenate(weights, axis=1))
+    tick_u(3 * g + 2)
+    tick_a(2 * g)
+    tick_a(2 * g + 1)
+    for stage in range(3):
+        @pl.when(g == stage + 1)
+        def _():
+            vec_total.step(stage)
+
+    @pl.when(g == steps - 1)
+    def _():
+        bias_total.copy(0).start()
+        out = pltpu.make_async_copy(total, gin_hbm, local_g)
+        out.start()
+        vec_total.step(3)
+        for extra in range(5):
+            tick_a(jnp.int32(CHUNKS + extra))
+            bias_total.step(extra)
+            if extra == 0:
+                vec_total.step(4)
+        vec_out[...] = vec_sums[5]
+        bias_out[...] = bias_sums[5]
+        for m in range(CHUNKS - 2, CHUNKS):
+            pair.copy(m).wait_send()
+
+        @pl.loop(0, CHUNKS)
+        def _(m):
+            scatter_u.drain(m)
+            scatter_a.drain(m)
+
+        vec_total.drain()
+        bias_total.drain()
+        out.wait()
+
+
+def attend_backward(grad_attended, tokens, keep_up, grad_one, vectors, own, other):
+    rows, depth = tokens.shape
+    width = own[0].shape[1]
+    steps = width // 128
+    inner = keep_up.shape[0] * keep_up.shape[4]
+    fixed = lambda *shape: pl.BlockSpec(shape, lambda g: (0,) * len(shape))
+    anywhere = pl.BlockSpec(memory_space=pl.ANY)
+    column = pl.BlockSpec((rows, 128), lambda g: (0, g))
+    side = [column] * 4 + [
+        pl.BlockSpec((128, depth), lambda g: (g, 0)),
+        pl.BlockSpec((3, depth, 128), lambda g: (0, 0, g)),
+    ]
+    sems = pltpu.SemaphoreType.DMA((5, CHUNKS))
+    few = pltpu.SemaphoreType.DMA((5,))
+    n_vec = vectors.shape[0]
+    f32 = jnp.float32
+    return pl.pallas_call(
+        attend_back_kernel,
+        grid=(steps,),
+        in_specs=[
+            fixed(rows, depth), fixed(rows, depth), anywhere, anywhere, fixed(n_vec, 128),
+            fixed(*own[4].shape), fixed(*other[4].shape),
+        ] + side + side,
+        out_specs=[
+            anywhere, fixed(depth // 16, inner), fixed(width, depth // 16),
+            fixed(3, depth // 16, width), fixed(n_vec, 128), fixed(16, 128),
+        ],
+        out_shape=[
+            jax.ShapeDtypeStruct((rows, depth), f32),
+            jax.ShapeDtypeStruct((depth // 16, inner), f32),
+            jax.ShapeDtypeStruct((width, depth // 16), f32),
+            jax.ShapeDtypeStruct((3, depth // 16, width), f32),
+            jax.ShapeDtypeStruct((n_vec, 128), f32),
+            jax.ShapeDtypeStruct((16, 128), f32),
+        ],
+        scratch_shapes=[
+            pltpu.VMEM((depth, rows), jnp.bfloat16),
+            pltpu.VMEM((depth, rows), jnp.bfloat16),
+            pltpu.VMEM((rows, depth), f32),
+            pltpu.VMEM((rows, 768), jnp.bfloat16),
+            *scatter_scratch(CHUNKS, SPAN, 256, False),
+            *land_scratch(CHUNKS, SPAN, 256),
+            *scatter_scratch(CHUNKS, SPAN, 256, True),
+            *land_scratch(CHUNKS, SPAN, 256),
+            pltpu.VMEM((6, n_vec, 128), f32),
+            pltpu.VMEM((5, n_vec, 128), f32),
+            pltpu.VMEM((6, 16, 128), f32),
+            pltpu.VMEM((5, 16, 128), f32),
+            sems, sems, sems, sems, few, few, few, few,
+            pltpu.SemaphoreType.DMA((CHUNKS,)),
+            pltpu.SemaphoreType.DMA,
+            pltpu.SemaphoreType.DMA,
+        ],
+        compiler_params=pltpu.CompilerParams(
+            vmem_limit_bytes=VMEM, collective_id=2, has_side_effects=True
+        ),
+        cost_estimate=pl.CostEstimate(
+            flops=rows * depth * width * 40, bytes_accessed=60 * 1024 * 1024, transcendentals=0
+        ),
+        name="attend_backward",
+    )(
+        grad_attended, tokens, keep_up, grad_one, vectors, own[4], other[4],
+        *own[:4], own[5], own[6], *other[:4], other[5], other[6],
+    )
+
+
+def body(mesh, *args):
+    tokens, w_qkv = args[0], args[2]
+    n_dp, n_tensor = mesh.shape["dp"], mesh.shape["tensor"]
+    local = (tokens.shape[0] % SEQ, w_qkv.shape[2], args[9].shape[1])
+    if (n_dp, n_tensor) == (16, 2) and local == (0, 512, 2048):
+        return body_tokens(*args)
+    return body_tensor(*args)
+
+
+def body_tokens(
+    tokens,
+    cotangent,
+    w_qkv,
+    bias_q,
+    bias_v,
+    w_out,
+    bias_o,
+    gain_one,
+    shift_one,
+    w_up,
+    bias_up,
+    w_down,
+    bias_down,
+    gain_two,
+    shift_two,
+):
+    me_dp, me_t = lax.axis_index("dp"), lax.axis_index("tensor")
+    core = me_dp % 2
+
+    def swap(value, dp_bit=0, tensor_bit=0):
+        pairs = [
+            ((d * 2 + t), ((d ^ dp_bit) * 2 + (t ^ tensor_bit))) for d in range(16) for t in range(2)
+        ]
+        return lax.ppermute(value, AXES, pairs)
+
+    def other_half(weight, axis):
+        size = weight.shape[axis] // 2
+        mine = lax.dynamic_slice_in_dim(weight, core * size, size, axis)
+        mine = swap(mine, tensor_bit=1)
+        theirs = swap(mine, dp_bit=1)
+        return jnp.where(
+            core == 0,
+            jnp.concatenate([mine, theirs], axis),
+            jnp.concatenate([theirs, mine], axis),
+        )
+
+    widths = (bias_q.shape[0], bias_v.shape[0], bias_up.shape[0])
+    biases = swap(jnp.concatenate([bias_q, bias_v, bias_up]), tensor_bit=1)
+    bias_q2 = biases[: widths[0]]
+    bias_v2 = biases[widths[0] : widths[0] + widths[1]]
+    bias_up2 = biases[widths[0] + widths[1] :]
+    w_qkv2 = other_half(w_qkv, 1)
+    w_out2 = other_half(w_out, 0)
+    w_up2 = other_half(w_up, 0)
+    w_down2 = other_half(w_down, 0)
+
+    halves = ((w_qkv, bias_q, bias_v), (w_qkv2, bias_q2, bias_v2))
+    kept = []
+    for weight, b_q, b_v in halves:
+        queries = (dot(tokens, weight[0]) + b_q).astype(jnp.bfloat16)
+        key_rows = dot(tokens, weight[1]).astype(jnp.bfloat16)
+        values = (dot(tokens, weight[2]) + b_v).astype(jnp.bfloat16)
+        context, level = attend_forward(queries, key_rows, values)
+        kept.append((queries, key_rows, values, level, context))
+    ctx, ctx2 = kept[0][4], kept[1][4]
+    attended = dot(ctx, w_out) + dot(ctx2, w_out2) + bias_o
+    hidden_one, normed_one, scaled_one = norm_forward(
+        tokens.astype(jnp.float32) + attended, gain_one, shift_one
+    )
+    hidden_rows = hidden_one.astype(jnp.bfloat16)
+
+    def expand(weight, bias):
+        activated, slope = gelu_pair(dot(hidden_rows, weight) + bias)
+        return activated.astype(jnp.bfloat16), slope.astype(jnp.bfloat16)
+
+    active, slope = expand(w_up, bias_up)
+    active2, slope2 = expand(w_up2, bias_up2)
+    branch = dot(active, w_down) + dot(active2, w_down2) + bias_down
+    result, normed_two, scaled_two = norm_forward(hidden_one + branch, gain_two, shift_two)
+    upstream = cotangent.astype(jnp.float32)
+    grad_two = norm_backward(upstream, gain_two, normed_two, scaled_two)
+    grad_branch = grad_two.astype(jnp.bfloat16)
+
+    grad_down, bias_up_parts, keep_up, raised = ffn_backward(
+        grad_branch, hidden_rows, active, active2, slope, slope2, w_down, w_down2, w_up, w_up2
+    )
+    grad_hidden = grad_two + raised
+    grad_one = norm_backward(grad_hidden, gain_one, normed_one, scaled_one)
+    grad_attended = grad_one.astype(jnp.bfloat16)
+    bias_parts = bias_up_parts.reshape(2, -1)
+    bias_parts = jnp.where(me_t == 0, bias_parts[::-1], bias_parts)
+    vectors = jnp.concatenate(
+        [
+            jnp.sum(upstream, axis=0),
+            jnp.sum(upstream * normed_two, axis=0),
+            jnp.sum(grad_branch.astype(jnp.float32), axis=0),
+            bias_parts.reshape(-1),
+            jnp.sum(grad_hidden, axis=0),
+            jnp.sum(grad_hidden * normed_one, axis=0),
+            jnp.sum(grad_attended.astype(jnp.float32), axis=0),
+        ]
+    )
+    (q1, k1, v1, l1, c1), (q2, k2, v2, l2, c2) = kept
+    grad_input, grad_up, grad_out, grad_qkv, vectors, biases = attend_backward(
+        grad_attended,
+        tokens,
+        keep_up,
+        grad_one,
+        vectors.reshape(-1, 128),
+        (q1, k1, v1, c1, l1, w_out, w_qkv),
+        (q2, k2, v2, c2, l2, w_out2, w_qkv2),
+    )
+    vectors = vectors.reshape(-1)
+    d, at, pieces = tokens.shape[1], 0, []
+    for size in (d, d, d, bias_parts.size, d, d, d):
+        pieces.append(vectors[at : at + size])
+        at += size
+    g_shift_two, g_gain_two, g_bias_down, g_bias_up, g_shift_one, g_gain_one, g_bias_o = pieces
+    g_bias_q, g_bias_v = biases[:8].reshape(-1), biases[8:].reshape(-1)
+    return (
+        result.astype(jnp.bfloat16),
+        grad_input,
+        grad_qkv,
+        g_bias_q,
+        g_bias_v,
+        grad_out,
+        g_bias_o,
+        g_gain_one,
+        g_shift_one,
+        grad_up,
+        g_bias_up,
+        grad_down,
+        g_bias_down,
+        g_gain_two,
+        g_shift_two,
+    )
+
+
 def solution(mesh):
     in_specs = (
         P(("dp", "tensor"), None),
@@ -251,4 +1026,4 @@
         P(),
         P(),
     )
-    return jax.shard_map(body, mesh=mesh, in_specs=in_specs, out_specs=out_specs, check_vma=False)
+    return jax.shard_map(functools.partial(body, mesh), mesh=mesh, in_specs=in_specs, out_specs=out_specs, check_vma=False)

time: 1130 us -> 461 us (0.41)
  waiting for transfers between devices: 659 us -> 106 us
  Pallas kernels: 0 us -> 225 us
  matrix products: 215 us -> 51.6 us
  local copies, waits for them, and re-layouts: 117 us -> 28.3 us
  blocking collectives: 41.4 us -> 0 us
  other arithmetic: 72.4 us -> 36.5 us
  between operations: 15.6 us -> 1.42 us
    reduce_scatter x7 -> x0, waiting for transfers between devices: 410 us -> none  [the longest x1 99.4 us: body(): lax.psum_scatter(jnp.dot(active_low, w_down, preferred_element_type=jnp.f...]
    pallas_call x0 -> x4, Pallas kernels: none -> 225 us  [the longest x1 125 us: attend_backward(): pl.pallas_call(attend_back_kernel, grid=(steps,), in_specs=[fixed(rows, d...]
    all_gather x4 -> x0, waiting for transfers between devices: 202 us -> none  [the longest x1 59.4 us: body(): full_rows = lax.all_gather(tokens, 'tensor', axis=0, tiled=True)]
    dot_general x40 -> x12, matrix products: 215 us -> 51.6 us  [dot(): return jnp.dot(left, right, preferred_element_type=jnp.float32)]
    ppermute x0 -> x9, waiting for transfers between devices: none -> 106 us  [swap(): return lax.ppermute(value, AXES, pairs)]
    unnamed x13 -> x0, waiting for transfers between devices: 47.5 us -> none
    another operation x13 -> x0, local copies, waits for them, and re-layouts: 43.1 us -> none  [the longest x7 36.9 us: body(): jnp.stack([grad_q.reshape(group_rows, local_width), grad_k.reshape(group_...]
    psum x1 -> x0, blocking collectives: 41.4 us -> none  [body(): lax.psum((placed(jnp.sum(grad_stack[0].astype(jnp.float32), axis=0), D),...]
  transfers between devices with their start and end apart: 12 -> 9, of which waited for: 10 -> 2; matrix products, arithmetic and copies ran while one was open for 18% -> 14% of each run, Pallas kernels for 0% -> 5%
where the time goes in v2:
time: 461 us; the launch traced here: 457 us
  Pallas kernels  225 us (49%)
  waiting for transfers between devices  106 us (23%)
  matrix products  51.6 us (11%)
  other arithmetic  36.5 us (8%)
  local copies, waits for them, and re-layouts  28.3 us (6%)
  starting transfers between devices  7.7 us (2%)
    pallas_call x1, Pallas kernels, attend_backward(): pl.pallas_call(attend_back_kernel, grid=(steps,), in_specs=[fixed(rows, d...  125 us
    ppermute x9, waiting for transfers between devices, swap(): return lax.ppermute(value, AXES, pairs)  106 us
    pallas_call x1, Pallas kernels, ffn_backward(): pl.pallas_call(ffn_back_kernel, grid=(CHUNKS,), in_specs=[whole, whole, c...  78.7 us
    dot_general x12, matrix products, dot(): return jnp.dot(left, right, preferred_element_type=jnp.float32)  51.6 us
    pallas_call x2, Pallas kernels, attend_forward(): pl.pallas_call(attend_kernel, grid=(seqs, groups), in_specs=[spec] * 3, o...  21.6 us
    select_n x4, other arithmetic, other_half(): jnp.where(core == 0, jnp.concatenate([mine, theirs], axis), jnp.concatena...  15.4 us
    unnamed x76, local copies, waits for them, and re-layouts  14.9 us
  transfers between devices with their start and end apart: 9, of which 2 were waited for; matrix products, arithmetic and copies ran while one was open for 14% of the time, Pallas kernels for 5%

profile of v2, /device:TPU:0, one launch (start us, length us, event | category | flops | bytes accessed | tf_op | source)
XLA Modules:
  0.0 456.7 jit_solution(13138361836427655215)
XLA Ops:
  0.7 2.7 constant_dynamic-slice_fusion.3
  3.3 3.0 collective-permute-start
  6.3 0.7 pad_maximum_fusion
  7.0 0.0 copy-start.16
  7.1 0.0 copy-start.8
  7.1 0.0 copy-start.26
  7.1 3.3 constant_dynamic-slice_fusion
  10.3 2.0 collective-permute-start.7
  12.3 3.2 constant_dynamic-slice_fusion.1
  15.5 0.1 collective-permute-start.5
  15.6 0.0 copy-start.13
  15.6 2.0 collective-permute-start.3
  17.6 3.5 add_convert_fusion.4.q_ref.q_own
  21.2 20.7 %collective-permute-done = bf16[3,512,512]{2,1,0:T(8,128)(2,1)} collective-permute-done((bf16[3,512,512]{2,1,0:T(8,128)(2,1)}, bf16[3,512,512]{2,1,0:T(8,128)(2,1)}, u32[]{:S(2)}, u32[]{:S(2)}) %collective-permute-start) | collective-permute-done | bytes 1572896 | tf_op jit(solution)/shard_map/ppermute | solution.py:889
  41.8 2.2 convolution_convert_fusion.1.k_ref.k_own
  44.0 2.2 add_convert_fusion.3.v_ref.v_own
  46.2 10.8 %attend_forward.2 = (bf16[1024,512]{1,0:T(8,128)(2,1)}, f32[2,8,512]{2,1,0:T(8,128)}) custom-call(bf16[1024,512]{1,0:T(8,128)(2,1)} %add_convert_fusion.4.q_ref.q_own, bf16[1024,512]{1,0:T(8,128)(2,1)} %convolution_convert_fusion.1.k_ref.k_own, bf16[1024,512]{1,0:T(8,128)(2,1)} %add_convert_fusion.3.v_ref.v_own), custom_call_target="tpu_custom_call" | custom-call | flops 1073741824 | bytes 4194304 | tf_op jit(solution)/shard_map/attend_forward/pallas_call | solution.py:271
  57.1 85.2 %collective-permute-done.3 = bf16[256,1024]{1,0:T(8,128)(2,1)S(1)} collective-permute-done((bf16[256,1024]{1,0:T(8,128)(2,1)S(1)}, bf16[256,1024]{1,0:T(8,128)(2,1)S(1)}, u32[]{:S(2)}, u32[]{:S(2)}) %collective-permute-start.3) | collective-permute-done | bytes 524320 | tf_op jit(solution)/shard_map/ppermute | solution.py:889
  142.3 4.5 fusion.36
  146.8 0.0 copy-start.9
  146.8 1.8 maximum_select_fusion.3.wo_oth
  148.6 0.6 collective-permute-start.8
  149.2 0.1 collective-permute-start.6
  149.3 3.3 maximum_select_fusion.2.wq_oth
  152.6 2.3 fusion.18.k_ref.k_oth
  154.9 2.2 fusion.20.v_ref.v_oth
  157.1 2.2 fusion.19.q_ref.q_oth
  159.4 10.8 %attend_forward.3 = (bf16[1024,512]{1,0:T(8,128)(2,1)}, f32[2,8,512]{2,1,0:T(8,128)}) custom-call(bf16[1024,512]{1,0:T(8,128)(2,1)} %fusion.19.q_ref.q_oth, bf16[1024,512]{1,0:T(8,128)(2,1)} %fusion.18.k_ref.k_oth, bf16[1024,512]{1,0:T(8,128)(2,1)} %fusion.20.v_ref.v_oth), custom_call_target="tpu_custom_call" | custom-call | flops 1073741824 | bytes 4194304 | tf_op jit(solution)/shard_map/attend_forward/pallas_call | solution.py:271
  170.1 4.0 fusion.34
  174.2 0.0 copy-start.19
  174.2 0.0 copy-start.24
  174.2 0.6 multiply_reduce_fusion.3
  174.8 0.0 copy-start.11
  174.8 0.1 copy-done.19
  174.9 0.0 copy-done.24
  175.0 0.7 fusion.17.hr_ref
  175.7 2.2 copy-done.11
  177.9 9.1 %fusion.4 = (bf16[1024,2048]{1,0:T(8,128)(2,1)}, bf16[1024,2048]{1,0:T(8,128)(2,1)S(1)}) fusion(f32[2048]{0:T(1024)S(1)} %copy-done.22, bf16[1024,1024]{1,0:T(8,128)(2,1)S(1)} %fusion.17.hr_ref, bf16[1024,2048]{1,0:T(8,128)(2,1)S(1)} %copy-done.11), kind=kOutput, calls=%fused_computation.6 | convolution fusion | flops 4320133120 | bytes 14688256 | tf_op jit(solution)/shard_map/dot_general | solution.py:230
  187.0 4.5 fusion.37
  191.6 0.0 slice-start
  191.6 4.7 %maximum_select_fusion.wu_oth = bf16[1024,2048]{1,0:T(8,128)(2,1)S(1)} fusion(bf16[512,2048]{1,0:T(8,128)(2,1)} %collective-permute-done.6, bf16[512,2048]{1,0:T(8,128)(2,1)} %collective-permute-done.5, pred[]{:T(512)S(6)} %eq.6), kind=kLoop, calls=%fused_computation.26 | loop fusion | flops 18874368 | bytes 8388609 | tf_op jit(solution)/shard_map/jit(_where)/select_n | solution.py:896
  196.3 9.6 %fusion.9 = (bf16[1024,2048]{1,0:T(8,128)(2,1)}, bf16[1024,2048]{1,0:T(8,128)(2,1)S(1)}) fusion(f32[2048]{0:T(1024)S(1)} %slice-done, bf16[1024,1024]{1,0:T(8,128)(2,1)S(1)} %fusion.17.hr_ref, bf16[1024,2048]{1,0:T(8,128)(2,1)S(1)} %maximum_select_fusion.wu_oth), kind=kOutput, calls=%fused_computation.11 | convolution fusion | flops 4320133120 | bytes 14688256 | tf_op jit(solution)/shard_map/dot_general | solution.py:230
  205.9 5.6 %maximum_select_fusion.1.wd_oth = bf16[2048,1024]{1,0:T(8,128)(2,1)S(1)} fusion(bf16[1024,1024]{1,0:T(8,128)(2,1)} %collective-permute-done.8, bf16[1024,1024]{1,0:T(8,128)(2,1)} %collective-permute-done.7, pred[]{:T(512)S(6)} %eq.6), kind=kLoop, calls=%fused_computation.27 | loop fusion | flops 18874368 | bytes 8388609 | tf_op jit(solution)/shard_map/jit(_where)/select_n | solution.py:896
  211.6 5.1 %fusion.35 = (f32[1024]{0:T(1024)S(1)}, f32[1024,1024]{1,0:T(8,128)S(1)}) fusion(f32[1024]{0:T(1024)S(1)} %copy-done.29, f32[1024,1024]{1,0:T(8,128)S(1)} %fusion.37, bf16[1024,2048]{1,0:T(8,128)(2,1)S(1)} %get-tuple-element.73.g_oth, bf16[2048,1024]{1,0:T(8,128)(2,1)S(1)} %maximum_select_fusion.1.wd_oth, f32[1024]{0:T(1024)S(1)} %copy-done.24, ...), kind=kOutput, calls=%fused_computation.99 | convolution fusion | flops 4303354880 | bytes 20996096 | tf_op jit(solution)/shard_map/dot_general | solution.py:230
  216.7 0.0 copy-start.2
  216.7 0.0 copy-start.18
  216.7 0.6 multiply_reduce_fusion.2
  217.3 2.5 copy-done.2
  219.8 2.3 fusion.16
  222.1 2.5 convert_reduce_fusion.2
  224.6 78.7 %ffn_backward.1 = (f32[2048,64]{1,0:T(8,128)}, f32[2,8,256]{2,1,0:T(8,128)}, bf16[8,2,2,256,256]{4,3,2,1,0:T(8,128)(2,1)}, f32[1024,1024]{1,0:T(8,128)}) custom-call(bf16[1024,1024]{1,0:T(8,128)(2,1)} %get-tuple-element.70.dm_ref, bf16[1024,1024]{1,0:T(8,128)(2,1)} %copy-done.7, bf16[1024,2048]{1,0:T(8,128)(2,1)} %copy-done.30, ...), custom_call_target="tpu_custom_call" | custom-call | flops 34359738368 | bytes 62914560 | tf_op jit(solution)/shard_map/ffn_backward/pallas_call | solution.py:546
  303.3 7.9 %multiply_reduce_fusion = (f32[1024]{0:T(1024)S(1)}, f32[1024]{0:T(1024)S(1)}, f32[1024]{0:T(1024)S(1)}, f32[1024]{0:T(1024)S(1)}, f32[1024,1024]{1,0:T(8,128)}, /*index=5*/bf16[1024,1024]{1,0:T(8,128)(2,1)}) fusion(f32[1024,1024]{1,0:T(8,128)S(1)} %get-tuple-element.88, f32[1024]{0:T(1024)S(1)} %add_rsqrt_fusion.1, f32[1024]{0:T(1024)S(1)} %broadcast_multiply_fusion.5, ...), kind=kLoop, calls=%fused_computation.29 | loop fusion | flops 22016000 | bytes 21024768 | tf_op jit(solution)/shard_map/reduce_sum | solution.py:954
  311.3 0.4 rev.3
  311.8 5.8 %convert_reduce_fusion.1 = (f32[1024]{0:T(1024)S(1)}, bf16[1024,1024]{1,0:T(8,128)(2,1)}, f32[1024,1024]{1,0:T(8,128)}) fusion(f32[1024]{0:T(1024)S(1)} %broadcast_multiply_fusion, f32[1024,1024]{1,0:T(8,128)} %copy-done, f32[1024]{0:T(1024)S(1)} %broadcast_multiply_fusion.5, f32[1024]{0:T(1024)S(1)} %broadcast_multiply_fusion.1, ...), kind=kLoop, calls=%fused_computation.28 | loop fusion | flops 10484736 | bytes 14704640 | tf_op jit(solution)/shard_map/reduce_sum | solution.py:955
  317.6 0.6 copy-done.28
  318.2 125.1 %attend_backward.1 = (f32[1024,1024]{1,0:T(8,128)}, f32[64,2048]{1,0:T(8,128)}, f32[512,64]{1,0:T(8,128)}, f32[3,64,512]{2,1,0:T(8,128)}, f32[80,128]{1,0:T(8,128)}, /*index=5*/f32[16,128]{1,0:T(8,128)}) custom-call(bf16[1024,1024]{1,0:T(8,128)(2,1)} %get-tuple-element.67.da_ref, bf16[1024,1024]{1,0:T(8,128)(2,1)} %x_ref.1, ...), custom_call_target="tpu_custom_call" | custom-call | flops 21474836480 | bytes 62914560 | tf_op jit(solution)/shard_map/attend_backward/pallas_call | solution.py:806
  443.3 1.3 slice_bitcast_fusion.10
  444.6 1.3 slice_bitcast_fusion.11
  445.9 1.3 slice_bitcast_fusion.17
  447.2 1.7 copy.35
  449.0 1.1 copy.36
  450.1 4.9 %copy.53 = f32[1024,1024]{1,0:T(8,128)} copy(f32[1024,1024]{1,0:T(8,128)} %get-tuple-element.109) | data formatting | bytes 8388608
  454.9 0.7 copy.54
  455.7 0.8 copy.55
  (79 shorter events, 0.2 us)
Async XLA Ops:
  3.3 38.5 %collective-permute-start = (bf16[3,512,512]{2,1,0:T(8,128)(2,1)}, bf16[3,512,512]{2,1,0:T(8,128)(2,1)}, u32[]{:S(2)}, u32[]{:S(2)}) collective-permute-start(bf16[3,512,512]{2,1,0:T(8,128)(2,1)} %constant_dynamic-slice_fusion.3), channel_id=1, source_target_pairs={{0,1},{1,0},{2,3},{3,2},{4,5},{5,4},{6,7},{7,6},{8,9},{9,8},{10,11... | collective-permute-start | bytes 4718600 | tf_op jit(solution)/shard_map/ppermute | solution.py:889
  7.0 139.8 %collective-permute-start.2 = (f32[3072]{0:T(1024)S(1)}, f32[3072]{0:T(1024)S(1)}, u32[]{:S(2)}, u32[]{:S(2)}) collective-permute-start(f32[3072]{0:T(1024)S(1)} %pad_maximum_fusion), channel_id=1, source_target_pairs={{0,1},{1,0},{2,3},{3,2},{4,5},{5,4},{6,7},{7,6},{8,9},{9,8},{10,11... | collective-permute-start | bytes 36872 | tf_op jit(solution)/shard_map/ppermute | solution.py:889
  7.0 8.5 %copy-start.16 = (bf16[512,1024]{1,0:T(8,128)(2,1)S(1)}, bf16[512,1024]{1,0:T(8,128)(2,1)}, u32[]{:S(2)}) copy-start(bf16[512,1024]{1,0:T(8,128)(2,1)} %wo_own.1) | copy-start | bytes 3145732
  7.1 10.6 %copy-start.8 = (bf16[1024,1024]{1,0:T(8,128)(2,1)S(1)}, bf16[1024,1024]{1,0:T(8,128)(2,1)}, u32[]{:S(2)}) copy-start(bf16[1024,1024]{1,0:T(8,128)(2,1)} %x_ref.1) | copy-start | bytes 6291460
  7.1 10.6 %copy-start.26 = (f32[512]{0:T(512)S(1)}, f32[512]{0:T(512)}, u32[]{:S(2)}) copy-start(f32[512]{0:T(512)} %param.18) | copy-start | bytes 6148
  10.3 138.2 %collective-permute-start.7 = (bf16[1024,1024]{1,0:T(8,128)(2,1)}, bf16[1024,1024]{1,0:T(8,128)(2,1)}, u32[]{:S(2)}, u32[]{:S(2)}) collective-permute-start(bf16[1024,1024]{1,0:T(8,128)(2,1)} %constant_dynamic-slice_fusion), channel_id=1, source_target_pairs={{0,1},{1,0},{2,3},{3,2},{4,5},{5,4},{6,7},{7,6},{8,9},{9,8},{10,11... | collective-permute-start | bytes 6291464 | tf_op jit(solution)/shard_map/ppermute | solution.py:889
  15.5 133.7 %collective-permute-start.5 = (bf16[512,2048]{1,0:T(8,128)(2,1)}, bf16[512,2048]{1,0:T(8,128)(2,1)}, u32[]{:S(2)}, u32[]{:S(2)}) collective-permute-start(bf16[512,2048]{1,0:T(8,128)(2,1)} %constant_dynamic-slice_fusion.1), channel_id=1, source_target_pairs={{0,1},{1,0},{2,3},{3,2},{4,5},{5,4},{6,7},{7,6},{8,9},{9,8},{10,11... | collective-permute-start | bytes 6291464 | tf_op jit(solution)/shard_map/ppermute | solution.py:889
  15.6 26.3 %copy-start.13 = (bf16[3,1024,512]{2,1,0:T(8,128)(2,1)S(1)}, bf16[3,1024,512]{2,1,0:T(8,128)(2,1)}, u32[]{:S(2)}) copy-start(bf16[3,1024,512]{2,1,0:T(8,128)(2,1)} %wq_own.1) | copy-start | bytes 9437188
  15.6 126.7 %collective-permute-start.3 = (bf16[256,1024]{1,0:T(8,128)(2,1)S(1)}, bf16[256,1024]{1,0:T(8,128)(2,1)S(1)}, u32[]{:S(2)}, u32[]{:S(2)}) collective-permute-start(bf16[256,1024]{1,0:T(8,128)(2,1)S(1)} %constant_dynamic-slice_fusion.2), channel_id=1, source_target_pairs={{0,1},{1,0},{2,3},{3,2},{4,5},{5,4},{6,7},{7,6},{8,9},{9,8},{10,11... | collective-permute-start | bytes 1572872 | tf_op jit(solution)/shard_map/ppermute | solution.py:889
  21.2 22.9 %copy-start.27 = (f32[512]{0:T(512)S(1)}, f32[512]{0:T(512)}, u32[]{:S(2)}) copy-start(f32[512]{0:T(512)} %param.19) | copy-start | bytes 6148
  41.8 107.4 %collective-permute-start.1 = (bf16[3,512,512]{2,1,0:T(8,128)(2,1)}, bf16[3,512,512]{2,1,0:T(8,128)(2,1)}, u32[]{:S(2)}, u32[]{:S(2)}) collective-permute-start(bf16[3,512,512]{2,1,0:T(8,128)(2,1)} %collective-permute-done), channel_id=1, source_target_pairs={{0,2},{1,3},{2,0},{3,1},{4,6},{5,7},{6,4},{7,5},{8,10},{9,11},{10,... | collective-permute-start | bytes 4718600 | tf_op jit(solution)/shard_map/ppermute | solution.py:889
  46.2 96.0 %copy-start.17 = (bf16[512,1024]{1,0:T(8,128)(2,1)S(1)}, bf16[512,1024]{1,0:T(8,128)(2,1)}, u32[]{:S(2)}) copy-start(bf16[512,1024]{1,0:T(8,128)(2,1)} %wo_own.1) | copy-start | bytes 3145732
  142.3 4.5 collective-permute-start.4
  146.8 5.8 %copy-start.21 = (f32[3072]{0:T(1024)}, f32[3072]{0:T(1024)S(1)}, u32[]{:S(2)}) copy-start(f32[3072]{0:T(1024)S(1)} %collective-permute-done.2) | copy-start | bytes 36868
  146.8 5.8 %copy-start.9 = (bf16[1024,1024]{1,0:T(8,128)(2,1)S(1)}, bf16[1024,1024]{1,0:T(8,128)(2,1)}, u32[]{:S(2)}) copy-start(bf16[1024,1024]{1,0:T(8,128)(2,1)} %x_ref.1) | copy-start | bytes 6291460
  148.6 21.6 %copy-start.5 = (bf16[512,1024]{1,0:T(8,128)(2,1)}, bf16[512,1024]{1,0:T(8,128)(2,1)S(1)}, u32[]{:S(2)}) copy-start(bf16[512,1024]{1,0:T(8,128)(2,1)S(1)} %maximum_select_fusion.3.wo_oth) | copy-start | bytes 3145732
  148.6 57.3 %collective-permute-start.8 = (bf16[1024,1024]{1,0:T(8,128)(2,1)}, bf16[1024,1024]{1,0:T(8,128)(2,1)}, u32[]{:S(2)}, u32[]{:S(2)}) collective-permute-start(bf16[1024,1024]{1,0:T(8,128)(2,1)} %collective-permute-done.7), channel_id=1, source_target_pairs={{0,2},{1,3},{2,0},{3,1},{4,6},{5,7},{6,4},{7,5},{8,10},{9,11},{10,... | collective-permute-start | bytes 6291464 | tf_op jit(solution)/shard_map/ppermute | solution.py:889
  149.2 42.4 %collective-permute-start.6 = (bf16[512,2048]{1,0:T(8,128)(2,1)}, bf16[512,2048]{1,0:T(8,128)(2,1)}, u32[]{:S(2)}, u32[]{:S(2)}) collective-permute-start(bf16[512,2048]{1,0:T(8,128)(2,1)} %collective-permute-done.5), channel_id=1, source_target_pairs={{0,2},{1,3},{2,0},{3,1},{4,6},{5,7},{6,4},{7,5},{8,10},{9,11},{10,... | collective-permute-start | bytes 6291464 | tf_op jit(solution)/shard_map/ppermute | solution.py:889
  152.6 4.5 copy-start.6
  159.4 10.8 %copy-start.23 = (f32[1024]{0:T(1024)S(1)}, f32[1024]{0:T(1024)}, u32[]{:S(2)}) copy-start(f32[1024]{0:T(1024)} %param.21) | copy-start | bytes 12292
  174.2 129.1 %copy-start = (f32[1024,1024]{1,0:T(8,128)}, f32[1024,1024]{1,0:T(8,128)S(1)}, u32[]{:S(2)}) copy-start(f32[1024,1024]{1,0:T(8,128)S(1)} %get-tuple-element.88) | copy-start | bytes 12582916
  174.2 0.7 copy-start.19
  174.2 0.7 copy-start.24
  174.8 3.1 copy-start.11
  174.8 3.1 copy-start.22
  177.9 18.4 %copy-start.7 = (bf16[1024,1024]{1,0:T(8,128)(2,1)}, bf16[1024,1024]{1,0:T(8,128)(2,1)S(1)}, u32[]{:S(2)}) copy-start(bf16[1024,1024]{1,0:T(8,128)(2,1)S(1)} %fusion.17.hr_ref) | copy-start | bytes 6291460
  177.9 9.1 %copy-start.12 = (bf16[2048,1024]{1,0:T(8,128)(2,1)S(1)}, bf16[2048,1024]{1,0:T(8,128)(2,1)}, u32[]{:S(2)}) copy-start(bf16[2048,1024]{1,0:T(8,128)(2,1)} %wd_own.1) | copy-start | bytes 12582916
  187.0 4.5 copy-start.30
  191.6 4.8 %slice-start = ((f32[3072]{0:T(1024)}), f32[2048]{0:T(1024)S(1)}, s32[]{:S(2)}) async-start(f32[3072]{0:T(1024)} %copy-done.21), calls=%async_computation | async-start | bytes 16384 | tf_op jit(solution)/shard_map/slice | solution.py:906
  196.3 9.6 %copy-start.3 = (bf16[1024,2048]{1,0:T(8,128)(2,1)}, bf16[1024,2048]{1,0:T(8,128)(2,1)S(1)}, u32[]{:S(2)}) copy-start(bf16[1024,2048]{1,0:T(8,128)(2,1)S(1)} %maximum_select_fusion.wu_oth) | copy-start | bytes 12582916
  205.9 5.6 %copy-start.31 = (bf16[1024,2048]{1,0:T(8,128)(2,1)}, bf16[1024,2048]{1,0:T(8,128)(2,1)S(1)}, u32[]{:S(2)}) copy-start(bf16[1024,2048]{1,0:T(8,128)(2,1)S(1)} %get-tuple-element.73.g_oth) | copy-start | bytes 12582916
  205.9 5.6 %copy-start.29 = (f32[1024]{0:T(1024)S(1)}, f32[1024]{0:T(1024)}, u32[]{:S(2)}) copy-start(f32[1024]{0:T(1024)} %param.27) | copy-start | bytes 12292
  211.5 5.2 %copy-start.4 = (bf16[2048,1024]{1,0:T(8,128)(2,1)}, bf16[2048,1024]{1,0:T(8,128)(2,1)S(1)}, u32[]{:S(2)}) copy-start(bf16[2048,1024]{1,0:T(8,128)(2,1)S(1)} %maximum_select_fusion.1.wd_oth) | copy-start | bytes 12582916
  216.7 5.4 %copy-start.1 = (f32[1024,1024]{1,0:T(8,128)}, f32[1024,1024]{1,0:T(8,128)S(1)}, u32[]{:S(2)}) copy-start(f32[1024,1024]{1,0:T(8,128)S(1)} %get-tuple-element.90) | copy-start | bytes 12582916
  216.7 3.1 copy-start.2
  216.7 3.1 copy-start.18
  224.6 78.7 %copy-start.25 = (f32[1024]{0:T(1024)S(1)}, f32[1024]{0:T(1024)}, u32[]{:S(2)}) copy-start(f32[1024]{0:T(1024)} %param.29) | copy-start | bytes 12292
  303.3 7.9 %copy-start.20 = (f32[2,8,256]{2,1,0:T(8,128)S(1)}, f32[2,8,256]{2,1,0:T(8,128)}, u32[]{:S(2)}) copy-start(f32[2,8,256]{2,1,0:T(8,128)} %get-tuple-element.33) | copy-start | bytes 49156
  317.6 0.6 copy-start.28
  318.2 130.7 %copy-start.10 = (f32[2048,64]{1,0:T(8,128)S(1)}, f32[2048,64]{1,0:T(8,128)}, u32[]{:S(2)}) copy-start(f32[2048,64]{1,0:T(8,128)} %get-tuple-element.54) | copy-start | bytes 1572868
  450.1 4.9 %copy-start.15 = (f32[3,64,512]{2,1,0:T(8,128)S(1)}, f32[3,64,512]{2,1,0:T(8,128)}, u32[]{:S(2)}) copy-start(f32[3,64,512]{2,1,0:T(8,128)} %get-tuple-element.110) | copy-start | bytes 1179652
  450.1 5.6 %copy-start.14 = (f32[64,2048]{1,0:T(8,128)S(1)}, f32[64,2048]{1,0:T(8,128)}, u32[]{:S(2)}) copy-start(f32[64,2048]{1,0:T(8,128)} %get-tuple-element.117) | copy-start | bytes 1572868
